TPU v7x, 512 devices: a whole 4x8x8 slice. The times are simulated.
512 devices in a mesh: acq: 32 (over z, x_lo, core), col: 16 (over x_hi, y).
Axes of the slice: x: 4 (x_hi: 2, x_lo: 2; x = x_hi * 2 + x_lo), y: 8, z: 8, core: 2. Of those that a mesh axis runs over, the one named last changes fastest.
Arguments:
- samples: float32 [128, 2, 24, 2048], P('acq', None, None, 'col'), may hold values from -3 to 3, as said below
- pair_live: int32 [128, 12], replicated, may hold values from 0 to 1, as said below
Outputs:
- displacement: float32 [128, 2, 24, 2048], P('acq', None, None, 'col')
- residual: float32 [128, 12, 2, 24, 2048], P('acq', None, None, None, 'col')
Inputs may be any that keep to these rules, and one draw needn't show every extreme that they name: pair_live[e, k] is 0 wherever e + k + 1 >= 128, and 1 for k = 0 wherever e + 1 < 128. `samples`: every sample's magnitude lies between 0.3 and 3.
All inputs are finite; a program needn't handle non-finite values.
Results may differ from a plain program's by a relative error of at most 0.0003.
Values sent between devices are 32-bit elements; how exact they have to be, the bound alone decides.
A program may use at most 64 MiB of HBM per device.

v0:
```python
import jax
import jax.numpy as jnp
from jax import lax
from jax.sharding import PartitionSpec as P

LOOK_ROWS = 5
LOOK_COLS = 20


def extended_2(block, sides, width):
    for axis, dim in sides:
        count = lax.axis_size(axis)
        forward = [(i, i + 1) for i in range(count - 1)]
        backward = [(target, source) for source, target in forward]
        low = lax.ppermute(
            lax.slice_in_dim(block, block.shape[dim] - width, None, axis=dim), axis, forward
        )
        high = lax.ppermute(lax.slice_in_dim(block, 0, width, axis=dim), axis, backward)
        block = jnp.concatenate([low, block, high], axis=dim)
    return block


def shifted(value, axis, steps):
    count = lax.axis_size(axis)
    initial, last = (max(0, -steps), min(count, count - steps))
    return lax.ppermute(value, axis, [(source, source + steps) for source in range(initial, last)])


def row_sum(source):
    half_rows = (LOOK_ROWS - 1) // 2
    pad_spec = ((0, 0),) * (source.ndim - 2) + ((half_rows, half_rows), (0, 0))
    padded = jnp.pad(source, pad_spec)
    count_rows = source.shape[-2]
    total = padded[..., 0:count_rows, :]
    for offset in range(1, LOOK_ROWS):
        total = total + padded[..., offset : offset + count_rows, :]
    return total


def look_sum(source, box_matrix):
    summed = row_sum(source)
    lead_shape = summed.shape[:-1]
    flat_rows = summed.reshape(-1, summed.shape[-1])
    looked = jnp.dot(flat_rows, box_matrix, precision=lax.Precision.HIGHEST)
    return looked.reshape(lead_shape + (box_matrix.shape[1],))


def later_stack(source, lags, count):
    return jnp.stack(
        [source[lag_index + 1 : lag_index + 1 + count] for lag_index in range(lags)], axis=1
    )


def design_matrix(live):
    acq_total = live.shape[0]
    lags = live.shape[1]
    acq_pos = lax.broadcasted_iota(jnp.int32, (acq_total, lags, acq_total - 1), 0)
    lag_pos = lax.broadcasted_iota(jnp.int32, (acq_total, lags, acq_total - 1), 1)
    col_pos = lax.broadcasted_iota(jnp.int32, (acq_total, lags, acq_total - 1), 2)
    later_hit = (col_pos == acq_pos + lag_pos).astype(jnp.float32)
    first_hit = (col_pos == acq_pos - 1).astype(jnp.float32)
    live_float = (live > 0).astype(jnp.float32)
    return ((later_hit - first_hit) * live_float[:, :, None]).reshape(
        acq_total * lags, acq_total - 1
    )


def per_device(samples, pair_live):
    acq_local = samples.shape[0]
    lags = pair_live.shape[1]
    hops_needed = -(-lags // acq_local)
    band_length = acq_local * (1 + hops_needed)
    col_local = samples.shape[3]
    start_acq = lax.axis_index("acq") * acq_local
    local_live = lax.dynamic_slice_in_dim(pair_live, start_acq, acq_local, 0)
    extended = extended_2(samples, (("col", 3),), LOOK_COLS // 2)
    blocks = [extended]
    current = extended
    for step_index in range(hops_needed):
        current = shifted(current, "acq", -1)
        blocks.append(current)
    acq_band = jnp.concatenate(blocks, axis=0)
    real_band = acq_band[:, 0]
    imag_band = acq_band[:, 1]
    power_band = real_band * real_band + imag_band * imag_band
    real_own = real_band[:acq_local][:, None]
    imag_own = imag_band[:acq_local][:, None]
    real_later = later_stack(real_band, lags, acq_local)
    imag_later = later_stack(imag_band, lags, acq_local)
    cross = jnp.stack(
        [
            real_own * real_later + imag_own * imag_later,
            imag_own * real_later - real_own * imag_later,
        ],
        axis=2,
    )
    ext_cols = acq_band.shape[-1]
    pos_ext = lax.broadcasted_iota(jnp.int32, (ext_cols, col_local), 0)
    pos_out = lax.broadcasted_iota(jnp.int32, (ext_cols, col_local), 1)
    box_matrix = ((pos_ext >= pos_out) & (pos_ext < pos_out + LOOK_COLS)).astype(jnp.float32)
    cross_look = look_sum(cross, box_matrix)
    power_look = look_sum(power_band, box_matrix)
    own_look = power_look[:acq_local][:, None]
    later_look = later_stack(power_look, lags, acq_local)
    live_mask = (local_live > 0)[:, :, None, None]
    denominator = jnp.sqrt(jnp.where(live_mask, own_look * later_look, 1.0))
    observed = jnp.where(live_mask[:, :, None], cross_look / denominator[:, :, None], 0.0)
    flat_obs = observed.reshape(acq_local * lags, -1)
    design = design_matrix(pair_live)
    normal = jnp.dot(design.T, design, precision=lax.Precision.HIGHEST)
    factor = jnp.linalg.cholesky(normal)
    design_local = lax.dynamic_slice_in_dim(design, start_acq * lags, acq_local * lags, 0)
    solved = jax.scipy.linalg.cho_solve((factor, True), design_local.T)
    flat_coef = jnp.concatenate([jnp.zeros((1, acq_local * lags), jnp.float32), solved], axis=0)
    block_shape = observed.shape[2:]
    partial_terms = jnp.dot(flat_coef, flat_obs, precision=lax.Precision.HIGHEST)
    summed = lax.psum(partial_terms, "acq")
    padded_disp = jnp.concatenate(
        [summed, jnp.zeros((acq_local * hops_needed, summed.shape[1]), jnp.float32)], axis=0
    )
    disp_band = lax.dynamic_slice_in_dim(padded_disp, start_acq, band_length, 0).reshape(
        (band_length,) + block_shape
    )
    own_disp = disp_band[:acq_local]
    later_disp = later_stack(disp_band, lags, acq_local)
    residual = jnp.where(live_mask[:, :, None], observed - (later_disp - own_disp[:, None]), 0.0)
    return (own_disp, residual)


def solution(mesh):
    placed = (P("acq", None, None, "col"), P())
    return jax.shard_map(
        per_device,
        mesh=mesh,
        in_specs=placed,
        out_specs=(P("acq", None, None, "col"), P("acq", None, None, None, "col")),
        check_vma=False,
    )
```

profile of v0, /device:TPU:1, one launch (start us, length us, event | category | flops | bytes accessed | tf_op | source)
XLA Modules:
  0.0 332.4 jit_solution(16501830061985671510)
XLA Ops:
  7.2 0.0 all-reduce.6.cloned.1.call-start
  7.2 1.1 fusion.63
  8.3 4.0 %collective-permute-start = (f32[4,2,24,10]{3,2,1,0:T(8,128)S(1)}, f32[4,2,24,10]{3,2,1,0:T(8,128)S(1)}, u32[]{:S(2)}, u32[]{:S(2)}) collective-permute-start(f32[4,2,24,10]{3,2,1,0:T(8,128)S(1)} %get-tuple-element.62), channel_id=1, source_target_pairs={{0,1},{1,2},{2,3},{3,4},{4,5},{5,6},{6,7},{7,8},{8,9},{9,10},{10,1... | collective-permute-start | bytes 23048 | tf_op jit(solution)/shard_map/ppermute | solution.py:15
  12.3 1.3 collective-permute-start.1
  13.6 0.0 copy-start.1
  13.7 0.7 compare_convert_fusion
  14.4 0.8 constant_dynamic-slice_fusion
  15.2 0.1 copy.79
  15.3 0.1 copy.55
  15.4 0.9 convolution_bitcast_fusion
  16.3 0.1 copy.54
  16.4 11.6 %cholesky.16 = f32[127,127]{1,0:T(8,128)S(1)} custom-call(f32[127,127]{1,0:T(8,128)S(1)} %fusion.44), custom_call_target="Cholesky" | custom-call | tf_op jit(solution)/shard_map/jit(cholesky)/cholesky | solution.py:111
  28.1 0.6 compare_reduce_fusion
  28.7 0.7 fusion.39
  29.4 9.7 %custom-call.10 = f32[1,127,127]{1,2,0:T(8,128)S(1)} custom-call(f32[1,127,127]{2,1,0:T(8,128)S(1)} %fusion.39), custom_call_target="InvertDiagBlocksLowerTriangular" | custom-call | tf_op jit(solution)/shard_map/jit(_cho_solve)/triangular_solve | solution.py:113
  39.1 0.1 mul.105
  39.2 0.1 iota.103
  39.3 0.1 iota.104
  39.4 0.1 dynamic-slice.2
  39.5 0.1 dynamic-slice.1
  39.6 0.1 add.97
  39.7 0.1 dynamic-slice
  39.8 0.2 fusion.42
  40.0 0.2 fusion.40
  40.3 0.1 fusion.62
  40.4 6.0 %collective-permute-start.2 = (f32[4,2,24,148]{3,2,0,1:T(8,128)S(1)}, f32[4,2,24,148]{3,2,0,1:T(8,128)S(1)}, u32[]{:S(2)}, u32[]{:S(2)}) collective-permute-start(f32[4,2,24,148]{3,2,0,1:T(8,128)S(1)} %get-tuple-element.60), channel_id=1, source_target_pairs={{16,0},{32,16},{48,32},{64,48},{80,64},{96,80},{112,96},{128,112},... | collective-permute-start | bytes 341000 | tf_op jit(solution)/shard_map/ppermute | solution.py:26
  46.5 0.1 pad_maximum_fusion.2
  46.7 1.1 collective-permute-done.2
  47.9 2.1 collective-permute-start.3
  50.0 4.9 %collective-permute-done.3 = f32[4,2,24,148]{3,2,0,1:T(8,128)S(1)} collective-permute-done((f32[4,2,24,148]{3,2,0,1:T(8,128)S(1)}, f32[4,2,24,148]{3,2,0,1:T(8,128)S(1)}, u32[]{:S(2)}, u32[]{:S(2)}) %collective-permute-start.3) | collective-permute-done | bytes 113696 | tf_op jit(solution)/shard_map/ppermute | solution.py:26
  54.9 2.1 collective-permute-start.4
  57.1 4.7 %collective-permute-done.4 = f32[4,2,24,148]{3,2,1,0:T(8,128)S(1)} collective-permute-done((f32[4,2,24,148]{3,2,1,0:T(8,128)S(1)}, f32[4,2,24,148]{3,2,1,0:T(8,128)S(1)}, u32[]{:S(2)}, u32[]{:S(2)}) %collective-permute-start.4) | collective-permute-done | bytes 113696 | tf_op jit(solution)/shard_map/ppermute | solution.py:26
  61.9 0.2 pad_maximum_fusion.1
  62.0 0.1 fusion.21
  62.1 0.2 fusion.19
  62.3 0.3 fusion.45
  62.8 0.4 multiply_add_fusion
  63.2 0.2 pad_maximum_fusion
  63.5 0.2 select_sqrt_fusion
  63.7 2.1 fusion.9
  65.9 0.2 reshape.890
  66.1 4.4 %fusion.50 = f32[128,6144]{1,0:T(8,128)} fusion(f32[48,6144]{1,0:T(8,128)S(1)} %reshape.890, f32[127,48]{0,1:T(8,128)S(1)} %fusion.40), kind=kOutput, calls=%fused_computation.167 | convolution fusion | flops 452984832 | bytes 4349760 | tf_op jit(solution)/shard_map/dot_general | solution.py:116
  70.5 0.0 all-reduce.6.cloned.1.call-update
  70.5 250.5 %all-reduce.6.cloned.1.call-done = f32[128,6144]{1,0:T(8,128)} async-done(((f32[128,6144]{1,0:T(8,128)}), f32[128,6144]{1,0:T(8,128)}) %all-reduce.6.cloned.1.call-update) | async-done | bytes 3145744 | tf_op jit(solution)/shard_map/psum | solution.py:117
  321.0 2.4 fusion.24
  323.6 0.3 copy-done
  323.9 0.1 fusion.36
  324.3 1.2 subtract_select_fusion
  (67 shorter events, 0.7 us)
Async XLA Ops:
  7.2 313.8 %all-reduce.6.cloned.1.call-start = ((), (), s32[]{:S(2)}) async-start(), calls=%async_computation | async-start | bytes 6291456 | tf_op jit(solution)/shard_map/psum | solution.py:117
  8.3 32.0 %collective-permute-start = (f32[4,2,24,10]{3,2,1,0:T(8,128)S(1)}, f32[4,2,24,10]{3,2,1,0:T(8,128)S(1)}, u32[]{:S(2)}, u32[]{:S(2)}) collective-permute-start(f32[4,2,24,10]{3,2,1,0:T(8,128)S(1)} %get-tuple-element.62), channel_id=1, source_target_pairs={{0,1},{1,2},{2,3},{3,4},{4,5},{5,6},{6,7},{7,8},{8,9},{9,10},{10,1... | collective-permute-start | bytes 23048 | tf_op jit(solution)/shard_map/ppermute | solution.py:15
  12.3 28.0 %collective-permute-start.1 = (f32[4,2,24,10]{3,2,1,0:T(8,128)S(1)}, f32[4,2,24,10]{3,2,1,0:T(8,128)S(1)}, u32[]{:S(2)}, u32[]{:S(2)}) collective-permute-start(f32[4,2,24,10]{3,2,1,0:T(8,128)S(1)} %get-tuple-element.63), channel_id=1, source_target_pairs={{1,0},{2,1},{3,2},{4,3},{5,4},{6,5},{7,6},{8,7},{9,8},{10,9},{11,1... | collective-permute-start | bytes 23048 | tf_op jit(solution)/shard_map/ppermute | solution.py:18
  13.6 26.6 %copy-start.1 = (f32[4,2,24,128]{3,2,1,0:T(8,128)S(1)}, f32[4,2,24,128]{3,2,1,0:T(8,128)}, u32[]{:S(2)}) copy-start(f32[4,2,24,128]{3,2,1,0:T(8,128)} %param.2) | copy-start | bytes 294916
  40.4 7.3 %collective-permute-start.2 = (f32[4,2,24,148]{3,2,0,1:T(8,128)S(1)}, f32[4,2,24,148]{3,2,0,1:T(8,128)S(1)}, u32[]{:S(2)}, u32[]{:S(2)}) collective-permute-start(f32[4,2,24,148]{3,2,0,1:T(8,128)S(1)} %get-tuple-element.60), channel_id=1, source_target_pairs={{16,0},{32,16},{48,32},{64,48},{80,64},{96,80},{112,96},{128,112},... | collective-permute-start | bytes 341000 | tf_op jit(solution)/shard_map/ppermute | solution.py:26
  47.9 7.0 %collective-permute-start.3 = (f32[4,2,24,148]{3,2,0,1:T(8,128)S(1)}, f32[4,2,24,148]{3,2,0,1:T(8,128)S(1)}, u32[]{:S(2)}, u32[]{:S(2)}) collective-permute-start(f32[4,2,24,148]{3,2,0,1:T(8,128)S(1)} %collective-permute-done.2), channel_id=1, source_target_pairs={{16,0},{32,16},{48,32},{64,48},{80,64},{96,80},{112,96},{128,112},... | collective-permute-start | bytes 341000 | tf_op jit(solution)/shard_map/ppermute | solution.py:26
  54.9 7.0 %collective-permute-start.4 = (f32[4,2,24,148]{3,2,1,0:T(8,128)S(1)}, f32[4,2,24,148]{3,2,1,0:T(8,128)S(1)}, u32[]{:S(2)}, u32[]{:S(2)}) collective-permute-start(f32[4,2,24,148]{3,2,1,0:T(8,128)S(1)} %copy.59), channel_id=1, source_target_pairs={{16,0},{32,16},{48,32},{64,48},{80,64},{96,80},{112,96},{128,112},... | collective-permute-start | bytes 341000 | tf_op jit(solution)/shard_map/ppermute | solution.py:26
  321.0 2.8 copy-start
  324.1 1.4 copy-start.2
Sparse Core Ops, SparseCore 0:
  70.6 250.3 all-reduce.5
where the time goes:
time: 333 us; the launch traced here: 332 us
  waiting for transfers between devices  261 us (78%)
  other arithmetic  26.1 us (8%)
  starting transfers between devices  15.6 us (5%)
  between operations  14.7 us (4%)
  matrix products  8.26 us (2%)
  local copies, waits for them, and re-layouts  6.42 us (2%)
    psum x1, waiting for transfers between devices, per_device(): summed = lax.psum(partial_terms, 'acq')  250 us
    another operation x3, other arithmetic, per_device(): factor = jnp.linalg.cholesky(normal)  12.3 us
    ppermute x3, waiting for transfers between devices, shifted(): lax.ppermute(value, axis, [(source, source + steps) for source in range(i...  10.7 us
    another operation x2, other arithmetic, per_device(): solved = jax.scipy.linalg.cho_solve((factor, True), design_local.T)  10.4 us
    ppermute x3, starting transfers between devices, shifted(): lax.ppermute(value, axis, [(source, source + steps) for source in range(i...  10.2 us
  transfers between devices with their start and end apart: 6, of which 4 were waited for; matrix products, arithmetic and copies ran while one was open for 8% of the time, Pallas kernels for 0%

commit v1 on v0

v1 whole, which is shorter than its diff:
```python
import functools

import jax
import jax.numpy as jnp
from jax import lax
from jax.experimental import pallas as pl
from jax.experimental.pallas import tpu as pltpu
from jax.sharding import PartitionSpec as P

MESH = pl.DeviceIdType.MESH
F32 = jnp.float32
BF16 = jnp.bfloat16
LOCAL = 4
BAND = 16
LAGS = 12
ROWS = 24
COLS = 128
GROUP = 48
CHUNK = 384
HALO = 10


def rem(a, n):
    return lax.rem(a + 4 * n, n)


def iota(shape, dim):
    return lax.broadcasted_iota(jnp.int32, shape, dim)


def split(value):
    high = value.astype(BF16)
    return high, (value - high.astype(F32)).astype(BF16)


def normal_matrix(live):
    n = live.shape[0]
    row, col = iota((n, n), 0), iota((n, n), 1)
    upper = jnp.zeros((n, n), F32)
    for k in range(LAGS):
        weight = jnp.where(live[:, k : k + 1] > 0, 1.0, 0.0)
        upper = upper + jnp.where(col == row + (k + 1), weight, 0.0)
    both = upper + upper.T
    degree = jnp.sum(both, axis=1, keepdims=True)
    full = jnp.where(row == col, degree, -both)
    grounded = jnp.where((row == 0) & (col == 0), 1.0, 0.0)
    return jnp.where((row == 0) | (col == 0), grounded, full)


def gauss_jordan(matrix):
    n = matrix.shape[0]
    row, col = iota((n, n), 0), iota((n, n), 1)

    def group(_, a):
        for s in range(8):
            pivot = 1.0 / a[s : s + 1, s : s + 1]
            scaled = jnp.where(col[:1] == s, pivot, a[s : s + 1, :] * pivot)
            update = jnp.where(col == s, 0.0, a) - a[:, s : s + 1] * scaled
            a = jnp.where(row == s, scaled, update)
        a = jnp.concatenate([a[8:], a[:8]], axis=0)
        return pltpu.roll(a, n - 8, axis=1)

    inverse = lax.fori_loop(0, n // 8, group, matrix)
    return jnp.where((row == 0) | (col == 0), 0.0, inverse)


def box_weights():
    source, out = iota((COLS, COLS), 0), iota((COLS, COLS), 1)
    own = (source >= out - HALO) & (source < out + HALO)
    side = jnp.where(source >= 4 * HALO, source - 4 * HALO, source)
    for step in (2, 1):
        side = jnp.where(side >= step * HALO, side - step * HALO, side)
    left = (source < 4 * HALO) & (out <= side)
    right = (source >= 4 * HALO) & (source < 8 * HALO) & (out >= side + COLS - HALO + 1)
    return jnp.concatenate(
        [jnp.where(own, 1.0, 0.0), jnp.where(left | right, 1.0, 0.0)], axis=0
    ).astype(BF16)


def kernel(
    n_acq, n_col,
    x_ref, live_ref, live_smem, disp_ref, res_ref,
    main, edges, packed, lhs_hi, lhs_lo, hx_hi, hx_lo, weights, ypad, scale, obs, rhs,
    inverse, p2_send, p2_recv, odd, sol, p3_send, p3_recv,
    own_sem, main_send, main_recv, edge_send, edge_recv, p2_ss, p2_rs, p3_ss, p3_rs,
):
    me, col = lax.axis_index("acq"), lax.axis_index("col")
    left, right = rem(col - 1, n_col), rem(col + 1, n_col)
    lane = iota((ROWS, COLS), 1)

    own = pltpu.make_async_copy(x_ref, main.at[pl.ds(0, LOCAL)], own_sem)
    own.start()

    barrier = pltpu.get_barrier_semaphore()

    @pl.loop(1, n_acq)
    def _(i):
        pl.semaphore_signal(barrier, inc=1, device_id=(rem(me + i, n_acq), col), device_id_type=MESH)

    for side in (left, right):

        @pl.loop(-3, 4)
        def _(i):
            pl.semaphore_signal(barrier, inc=1, device_id=(rem(me + i, n_acq), side), device_id_type=MESH)

    own.wait()
    to_right = jnp.zeros((ROWS, COLS), F32)
    to_left = jnp.zeros((ROWS, COLS), F32)
    for m in range(2):
        for i in range(LOCAL):
            base = 4 * HALO * m + HALO * i
            hit = (lane >= base) & (lane < base + HALO)
            value = main[i, m]
            to_right = jnp.where(hit, pltpu.roll(value, (base + HALO) % COLS, axis=1), to_right)
            to_left = jnp.where(hit, pltpu.roll(value, base, axis=1) if base else value, to_left)
    packed[0] = to_right
    packed[1] = to_left

    pl.semaphore_wait(barrier, n_acq - 1 + 14)

    copies = []
    for i in range(1, 4):
        copies.append(
            pltpu.make_async_remote_copy(
                x_ref, main.at[pl.ds(LOCAL * i, LOCAL)], main_send.at[i], main_recv.at[i],
                device_id=(rem(me - i, n_acq), col), device_id_type=MESH,
            )
        )
    for i in range(4):
        for side, target in ((0, right), (1, left)):
            copies.append(
                pltpu.make_async_remote_copy(
                    packed.at[side], edges.at[i, side], edge_send.at[i, side], edge_recv.at[i, side],
                    device_id=(rem(me - i, n_acq), target), device_id_type=MESH,
                )
            )
    for copy in copies:
        copy.start()

    inverse[...] = gauss_jordan(normal_matrix(live_ref[...]))
    weights[...] = box_weights()
    ypad[...] = jnp.zeros(ypad.shape, F32)
    rhs[...] = jnp.zeros(rhs.shape, F32)

    for copy in copies:
        copy.wait()

    keep_left = jnp.where(col > 0, 1.0, 0.0)
    keep_right = jnp.where(col < n_col - 1, 1.0, 0.0)
    in_left = lane < 4 * HALO
    in_right = (lane >= 4 * HALO) & (lane < 8 * HALO)
    real, imag = [], []
    for b in range(4):
        low, high = edges[b, 0] * keep_left, edges[b, 1] * keep_right
        real.append(jnp.where(in_left, low, jnp.where(in_right, pltpu.roll(high, 4 * HALO, axis=1), 0.0)))
        imag.append(jnp.where(in_left, pltpu.roll(low, COLS - 4 * HALO, axis=1), jnp.where(in_right, high, 0.0)))
    side_lane = jnp.where(lane >= 4 * HALO, lane - 4 * HALO, lane)

    def later(parts, lag):
        b, s = divmod(lag, 4)
        if s == 0:
            return parts[b]
        return jnp.where(
            side_lane < HALO * (4 - s),
            pltpu.roll(parts[b], COLS - HALO * s, axis=1),
            pltpu.roll(parts[b + 1], HALO * (4 - s), axis=1),
        )

    for k in range(LAGS):
        later_re, later_im = later(real, k + 1), later(imag, k + 1)
        cross = jnp.concatenate(
            [
                real[0] * later_re + imag[0] * later_im,
                imag[0] * later_re - real[0] * later_im,
            ],
            axis=0,
        )
        hx_hi[k], hx_lo[k] = split(cross)

    def slot_of(lanes, i):
        place = jnp.where(lanes >= 4 * HALO, lanes - 4 * HALO, lanes)
        return (place >= HALO * i) & (place < HALO * (i + 1)) & (lanes < 8 * HALO)

    for b in range(4):
        edge_power = real[b] * real[b] + imag[b] * imag[b]
        for h in range(2):
            parts, sides = [], []
            for i in (2 * h, 2 * h + 1):
                re, im = main[LOCAL * b + i, 0], main[LOCAL * b + i, 1]
                parts.append(re * re + im * im)
                sides.append(jnp.where(slot_of(lane, i), edge_power, 0.0))
            at = pl.ds((2 * b + h) * GROUP, GROUP)
            lhs_hi[at, :COLS], lhs_lo[at, :COLS] = split(jnp.concatenate(parts, axis=0))
            lhs_hi[at, COLS:], lhs_lo[at, COLS:] = split(jnp.concatenate(sides, axis=0))

    lane_wide = iota((GROUP, COLS), 1)
    slots = [jnp.where(slot_of(lane_wide, i), 1.0, 0.0).astype(BF16) for i in range(LOCAL)]

    @pl.loop(0, LAGS)
    def _(k):
        side_hi, side_lo = hx_hi[k], hx_lo[k]
        for e in range(LOCAL):
            re, im = main[e, 0], main[e, 1]
            re_j, im_j = main[e + k + 1, 0], main[e + k + 1, 1]
            cross = jnp.concatenate([re * re_j + im * im_j, im * re_j - re * im_j], axis=0)
            at = pl.ds(pl.multiple_of(CHUNK + k * (LOCAL * GROUP) + e * GROUP, 16), GROUP)
            lhs_hi[at, :COLS], lhs_lo[at, :COLS] = split(cross)
            lhs_hi[at, COLS:] = side_hi * slots[e]
            lhs_lo[at, COLS:] = side_lo * slots[e]

    def looked(chunk):
        at = pl.ds(pl.multiple_of(chunk * CHUNK, 16), CHUNK)
        by_cols = jnp.dot(lhs_hi[at, :], weights[...], preferred_element_type=F32)
        by_cols = by_cols + jnp.dot(lhs_lo[at, :], weights[...], preferred_element_type=F32)
        ypad[:, 8 : 8 + ROWS, :] = by_cols.reshape(CHUNK // ROWS, ROWS, COLS)

        def one(i):
            total = ypad[i, 6 : 6 + ROWS, :]
            for t in range(1, 5):
                total = total + ypad[i, 6 + t : 6 + t + ROWS, :]
            return total

        return one

    power = looked(0)
    for i in range(BAND):
        scale[i] = lax.rsqrt(power(i))

    @pl.loop(1, LAGS // 2 + 1)
    def _(chunk):
        one = looked(chunk)
        for half in range(2):
            k = 2 * chunk - 2 + half
            for e in range(LOCAL):
                live = jnp.where(live_smem[LOCAL * me + e, k] > 0, 1.0, 0.0)
                factor = scale[e] * scale[e + k + 1] * live
                for m in range(2):
                    value = one((half * LOCAL + e) * 2 + m) * factor
                    obs[e, k, m] = value
                    rhs[m, e] = rhs[m, e] - value
                    rhs[m, e + k + 1] = rhs[m, e + k + 1] + value

    for m in range(2):
        for j in range(BAND):
            p2_send[pl.ds(BAND * m + j, ROWS, stride=2 * BAND), :] = rhs[m, j]

    z = me // 4
    turn = me - 4 * z - lax.rem(z, 2)
    is_owner = (turn >= 0) & (turn < 3)
    row_me = 3 * z + turn
    first = rem(3 * z, ROWS)
    size = 2 * BAND

    @pl.loop(0, ROWS)
    def _(i):
        r = rem(first + i, ROWS)
        zr = r // 3
        target = 4 * zr + (r - 3 * zr) + lax.rem(zr, 2)

        @pl.when(target != me)
        def _():
            pltpu.make_async_remote_copy(
                p2_send.at[pl.ds(pl.multiple_of(r * size, 8), size)],
                p2_recv.at[pl.ds(pl.multiple_of(me * size, 8), size)],
                p2_ss, p2_rs, device_id=(target, col), device_id_type=MESH,
            ).start()

    def wait(ref, blocks, sem):
        part = ref.at[pl.ds(0, blocks * size)]
        pltpu.make_async_copy(part, part, sem).wait()

    @pl.when(is_owner)
    def _():
        p2_recv[pl.ds(pl.multiple_of(me * size, 8), size), :] = p2_send[
            pl.ds(pl.multiple_of(row_me * size, 8), size), :
        ]
        wait(p2_recv, n_acq - 1, p2_rs)
        sums = []
        for m in range(2):

            def part(a, h):
                at = a * size + m * BAND + 8 * h
                return p2_recv[at : at + 8, :]

            odd[m, 0:8, :] = jnp.zeros((8, COLS), F32)
            for v in range(16):
                value = part(2 * v + 1, 0)
                if v:
                    value = value + part(2 * v - 1, 1)
                odd[m, 8 * v + 8 : 8 * v + 16, :] = value
            even = []
            for v in range(16):
                value = part(2 * v, 0)
                if v:
                    value = value + part(2 * v - 2, 1)
                even.append(value)
            sums.append(jnp.concatenate(even, axis=0) + odd[m, 4 : 4 + 128, :])
        solved = jnp.dot(
            inverse[...], jnp.concatenate(sums, axis=1),
            precision=lax.Precision.HIGHEST, preferred_element_type=F32,
        )
        for m in range(2):
            sol[m, 0:128, :] = solved[:, m * COLS : (m + 1) * COLS]
            sol[m, 128:144, :] = jnp.zeros((16, COLS), F32)
        for a in range(32):
            for m in range(2):
                at = a * size + m * BAND
                p3_send[at : at + BAND, :] = sol[m, 4 * a : 4 * a + BAND, :]

        @pl.loop(1, n_acq)
        def _(i):
            target = rem(me + i, n_acq)
            pltpu.make_async_remote_copy(
                p3_send.at[pl.ds(pl.multiple_of(target * size, 8), size)],
                p3_recv.at[pl.ds(pl.multiple_of(row_me * size, 8), size)],
                p3_ss, p3_rs, device_id=(target, col), device_id_type=MESH,
            ).start()

        p3_recv[pl.ds(pl.multiple_of(row_me * size, 8), size), :] = p3_send[
            pl.ds(pl.multiple_of(me * size, 8), size), :
        ]
        wait(p2_send, ROWS - 1, p2_ss)
        wait(p3_recv, ROWS - 1, p3_rs)
        wait(p3_send, n_acq - 1, p3_ss)

    @pl.when(jnp.logical_not(is_owner))
    def _():
        wait(p2_send, ROWS, p2_ss)
        wait(p3_recv, ROWS, p3_rs)

    for m in range(2):
        for j in range(BAND):
            rhs[m, j] = p3_recv[pl.ds(BAND * m + j, ROWS, stride=2 * BAND), :]
    for e in range(LOCAL):
        for m in range(2):
            disp_ref[e, m] = rhs[m, e]

    @pl.loop(0, LAGS)
    def _(k):
        for e in range(LOCAL):
            live = jnp.where(live_smem[LOCAL * me + e, k] > 0, 1.0, 0.0)
            for m in range(2):
                res_ref[e, k, m] = obs[e, k, m] - (rhs[m, e + k + 1] - rhs[m, e]) * live


def per_device(n_acq, n_col, samples, pair_live):
    vmem = pltpu.VMEM
    rows_all = CHUNK + LAGS * LOCAL * GROUP
    return pl.pallas_call(
        functools.partial(kernel, n_acq, n_col),
        out_shape=(
            jax.ShapeDtypeStruct((LOCAL, 2, ROWS, COLS), F32),
            jax.ShapeDtypeStruct((LOCAL, LAGS, 2, ROWS, COLS), F32),
        ),
        in_specs=[
            pl.BlockSpec(memory_space=pl.ANY),
            pl.BlockSpec(memory_space=pltpu.VMEM),
            pl.BlockSpec(memory_space=pltpu.SMEM),
        ],
        out_specs=(pl.BlockSpec(memory_space=pltpu.VMEM), pl.BlockSpec(memory_space=pltpu.VMEM)),
        scratch_shapes=[
            vmem((BAND, 2, ROWS, COLS), F32),
            vmem((4, 2, ROWS, COLS), F32),
            vmem((2, ROWS, COLS), F32),
            vmem((rows_all, 2 * COLS), BF16),
            vmem((rows_all, 2 * COLS), BF16),
            vmem((LAGS, GROUP, COLS), BF16),
            vmem((LAGS, GROUP, COLS), BF16),
            vmem((2 * COLS, COLS), BF16),
            vmem((CHUNK // ROWS, 40, COLS), F32),
            vmem((BAND, ROWS, COLS), F32),
            vmem((LOCAL, LAGS, 2, ROWS, COLS), F32),
            vmem((2, BAND, ROWS, COLS), F32),
            vmem((128, 128), F32),
            vmem((ROWS * 2 * BAND, COLS), F32),
            vmem((n_acq * 2 * BAND, COLS), F32),
            vmem((2, 136, COLS), F32),
            vmem((2, 144, COLS), F32),
            vmem((n_acq * 2 * BAND, COLS), F32),
            vmem((ROWS * 2 * BAND, COLS), F32),
            pltpu.SemaphoreType.DMA,
            pltpu.SemaphoreType.DMA((4,)),
            pltpu.SemaphoreType.DMA((4,)),
            pltpu.SemaphoreType.DMA((4, 2)),
            pltpu.SemaphoreType.DMA((4, 2)),
            pltpu.SemaphoreType.DMA,
            pltpu.SemaphoreType.DMA,
            pltpu.SemaphoreType.DMA,
            pltpu.SemaphoreType.DMA,
        ],
        compiler_params=pltpu.CompilerParams(
            collective_id=0, has_side_effects=True, vmem_limit_bytes=32 * 1024 * 1024
        ),
    )(samples, pair_live, pair_live)


def solution(mesh):
    return jax.shard_map(
        functools.partial(per_device, mesh.shape["acq"], mesh.shape["col"]),
        mesh=mesh,
        in_specs=(P("acq", None, None, "col"), P()),
        out_specs=(P("acq", None, None, "col"), P("acq", None, None, None, "col")),
        check_vma=False,
    )
```

time: 333 us -> 63.5 us (0.19)
  waiting for transfers between devices: 261 us -> 0 us
  Pallas kernels: 0 us -> 59.4 us
  other arithmetic: 26.1 us -> 0 us
  starting transfers between devices: 15.6 us -> 0 us
  between operations: 14.7 us -> 0.64 us
  matrix products: 8.26 us -> 0 us
    psum x1 -> x0, waiting for transfers between devices: 250 us -> none  [per_device(): summed = lax.psum(partial_terms, 'acq')]
    pallas_call x0 -> x1, Pallas kernels: none -> 59.4 us  [per_device(): pl.pallas_call(functools.partial(kernel, n_acq, n_col), out_shape=(jax.Sh...]
    another operation x6 -> x0, other arithmetic: 22.8 us -> none  [the longest x3 12.3 us: per_device(): factor = jnp.linalg.cholesky(normal)]
    ppermute x5 -> x0, starting transfers between devices: 15.6 us -> none  [the longest x3 10.2 us: shifted(): lax.ppermute(value, axis, [(source, source + steps) for source in range(i...]
    ppermute x5 -> x0, waiting for transfers between devices: 10.7 us -> none  [the longest x3 10.7 us: shifted(): lax.ppermute(value, axis, [(source, source + steps) for source in range(i...]
    dot_general x4 -> x0, matrix products: 7.8 us -> none  [the longest x1 4.42 us: per_device(): jnp.dot(flat_coef, flat_obs, precision=lax.Precision.HIGHEST)]
  transfers between devices with their start and end apart: 6 -> 0, of which waited for: 4 -> 0; matrix products, arithmetic and copies ran while one was open for 8% -> 0% of each run, Pallas kernels for 0% -> 0%
where the time goes in v1:
time: 63.5 us; the launch traced here: 63.3 us
  Pallas kernels  59.4 us (94%)
  local copies, waits for them, and re-layouts  3.35 us (5%)
  between operations  0.64 us (1%)
    pallas_call x1, Pallas kernels, per_device(): pl.pallas_call(functools.partial(kernel, n_acq, n_col), out_shape=(jax.Sh...  59.4 us
    unnamed x5, local copies, waits for them, and re-layouts  3.35 us

profile of v1, /device:TPU:1, one launch (start us, length us, event | category | flops | bytes accessed | tf_op | source)
XLA Modules:
  0.0 63.3 jit_solution(5764435828218675136)
XLA Ops:
  0.6 0.8 %copy.4.live_ref.live_smem = s32[128,12]{1,0:T(8,128)S(1)} copy(s32[128,12]{0,1:T(8,128)} %param.3) | data formatting | bytes 12288 | tf_op args[1]
  1.4 0.0 copy-start
  1.4 0.9 %copy-done = f32[4,2,24,128]{3,2,1,0:T(8,128)S(1)} copy-done((f32[4,2,24,128]{3,2,1,0:T(8,128)S(1)}, f32[4,2,24,128]{3,2,1,0:T(8,128)}, u32[]{:S(2)}) %copy-start) | copy-done | bytes 98328
  2.3 59.4 %shard_map.41 = (f32[4,2,24,128]{3,2,1,0:T(8,128)S(1)}, f32[4,12,2,24,128]{4,3,2,1,0:T(8,128)S(1)}) custom-call(f32[4,2,24,128]{3,2,1,0:T(8,128)S(1)} %copy-done, s32[128,12]{1,0:T(8,128)S(1)} %copy.4.live_ref.live_smem, s32[128,12]{1,0:T(8,128)S(1)} %copy.4.live_ref.live_smem), custom_call_target="tpu_custom_call" | custom-call | tf_op jit(solution)/shard_map/pallas_call | solution.py:349
  61.7 0.6 %copy.8 = f32[4,2,24,128]{3,2,1,0:T(8,128)} copy(f32[4,2,24,128]{3,2,1,0:T(8,128)S(1)} %get-tuple-element.4) | data formatting | bytes 196608
  62.3 1.0 %copy.9 = f32[4,12,2,24,128]{4,3,2,1,0:T(8,128)} copy(f32[4,12,2,24,128]{4,3,2,1,0:T(8,128)S(1)} %get-tuple-element.5) | data formatting | bytes 2359296
Async XLA Ops:
  1.4 0.9 %copy-start = (f32[4,2,24,128]{3,2,1,0:T(8,128)S(1)}, f32[4,2,24,128]{3,2,1,0:T(8,128)}, u32[]{:S(2)}) copy-start(f32[4,2,24,128]{3,2,1,0:T(8,128)} %x_ref.1) | copy-start | bytes 294916

commit v2 on v1

--- a/solution.py
+++ b/solution.py
@@ -18,6 +18,8 @@
 GROUP = 48
 CHUNK = 384
 HALO = 10
+WINDOW = 2 * BAND
+WIDE = 40
 
 
 def rem(a, n):
@@ -34,20 +36,20 @@
 
 
 def normal_matrix(live):
-    n = live.shape[0]
+    n = live.shape[1]
     row, col = iota((n, n), 0), iota((n, n), 1)
-    upper = jnp.zeros((n, n), F32)
+    lower = jnp.zeros((n, n), F32)
     for k in range(LAGS):
-        weight = jnp.where(live[:, k : k + 1] > 0, 1.0, 0.0)
-        upper = upper + jnp.where(col == row + (k + 1), weight, 0.0)
-    both = upper + upper.T
+        weight = jnp.where(live[k : k + 1, :] > 0, 1.0, 0.0)
+        lower = lower + jnp.where(row == col + (k + 1), weight, 0.0)
+    both = lower + lower.T
     degree = jnp.sum(both, axis=1, keepdims=True)
     full = jnp.where(row == col, degree, -both)
     grounded = jnp.where((row == 0) & (col == 0), 1.0, 0.0)
     return jnp.where((row == 0) | (col == 0), grounded, full)
 
 
-def gauss_jordan(matrix):
+def eliminate(matrix, groups):
     n = matrix.shape[0]
     row, col = iota((n, n), 0), iota((n, n), 1)
 
@@ -60,7 +62,11 @@
         a = jnp.concatenate([a[8:], a[:8]], axis=0)
         return pltpu.roll(a, n - 8, axis=1)
 
-    inverse = lax.fori_loop(0, n // 8, group, matrix)
+    return lax.fori_loop(0, groups, group, matrix)
+
+
+def ungrounded(inverse):
+    row, col = iota(inverse.shape, 0), iota(inverse.shape, 1)
     return jnp.where((row == 0) | (col == 0), 0.0, inverse)
 
 
@@ -81,8 +87,8 @@
     n_acq, n_col,
     x_ref, live_ref, live_smem, disp_ref, res_ref,
     main, edges, packed, lhs_hi, lhs_lo, hx_hi, hx_lo, weights, ypad, scale, obs, rhs,
-    inverse, p2_send, p2_recv, odd, sol, p3_send, p3_recv,
-    own_sem, main_send, main_recv, edge_send, edge_recv, p2_ss, p2_rs, p3_ss, p3_rs,
+    inverse, p2_send, p2_sib, p2_chip, p2_recv, sol, p3_recv,
+    own_sem, main_send, main_recv, edge_send, edge_recv, sib_ss, sib_rs, p2_ss, p2_rs, p3_ss, p3_rs, fw_ss, fw_rs,
 ):
     me, col = lax.axis_index("acq"), lax.axis_index("col")
     left, right = rem(col - 1, n_col), rem(col + 1, n_col)
@@ -93,9 +99,15 @@
 
     barrier = pltpu.get_barrier_semaphore()
 
-    @pl.loop(1, n_acq)
+    def greet(target):
+        pl.semaphore_signal(barrier, inc=1, device_id=(target, col), device_id_type=MESH)
+
+    for i in (1, -1, 3, -3):
+        greet(rem(me + i, n_acq))
+
+    @pl.loop(1, n_acq // 2)
     def _(i):
-        pl.semaphore_signal(barrier, inc=1, device_id=(rem(me + i, n_acq), col), device_id_type=MESH)
+        greet(rem(me + 2 * i, n_acq))
 
     for side in (left, right):
 
@@ -116,7 +128,7 @@
     packed[0] = to_right
     packed[1] = to_left
 
-    pl.semaphore_wait(barrier, n_acq - 1 + 14)
+    pl.semaphore_wait(barrier, 4 + n_acq // 2 - 1 + 14)
 
     copies = []
     for i in range(1, 4):
@@ -137,7 +149,7 @@
     for copy in copies:
         copy.start()
 
-    inverse[...] = gauss_jordan(normal_matrix(live_ref[...]))
+    inverse[...] = eliminate(normal_matrix(live_ref[...]), 8)
     weights[...] = box_weights()
     ypad[...] = jnp.zeros(ypad.shape, F32)
     rhs[...] = jnp.zeros(rhs.shape, F32)
@@ -232,7 +244,7 @@
         for half in range(2):
             k = 2 * chunk - 2 + half
             for e in range(LOCAL):
-                live = jnp.where(live_smem[LOCAL * me + e, k] > 0, 1.0, 0.0)
+                live = jnp.where(live_smem[k, LOCAL * me + e] > 0, 1.0, 0.0)
                 factor = scale[e] * scale[e + k + 1] * live
                 for m in range(2):
                     value = one((half * LOCAL + e) * 2 + m) * factor
@@ -242,95 +254,142 @@
 
     for m in range(2):
         for j in range(BAND):
-            p2_send[pl.ds(BAND * m + j, ROWS, stride=2 * BAND), :] = rhs[m, j]
-
-    z = me // 4
-    turn = me - 4 * z - lax.rem(z, 2)
-    is_owner = (turn >= 0) & (turn < 3)
-    row_me = 3 * z + turn
-    first = rem(3 * z, ROWS)
-    size = 2 * BAND
-
-    @pl.loop(0, ROWS)
-    def _(i):
-        r = rem(first + i, ROWS)
-        zr = r // 3
-        target = 4 * zr + (r - 3 * zr) + lax.rem(zr, 2)
-
-        @pl.when(target != me)
-        def _():
-            pltpu.make_async_remote_copy(
-                p2_send.at[pl.ds(pl.multiple_of(r * size, 8), size)],
-                p2_recv.at[pl.ds(pl.multiple_of(me * size, 8), size)],
-                p2_ss, p2_rs, device_id=(target, col), device_id_type=MESH,
-            ).start()
+            p2_send[pl.ds(8 * (j // 4) + 4 * m + j % 4, ROWS, stride=WINDOW), :] = rhs[m, j]
+
+    core = lax.rem(me, 2)
+    chip = me // 2
+    z, x = chip // 2, lax.rem(chip, 2)
+    sibling = me + 1 - 2 * core
+    planes = n_acq // 4
+    half = ROWS // 2
+
+    def place(zt, xt):
+        both = lax.rem(zt, 2) == core
+        return both | (xt == lax.rem(zt // 2 + core, 2)), 3 * (zt // 2) + jnp.where(both, xt, 2)
+
+    def plane(turn):
+        away = (planes - turn) // 2
+        return rem(jnp.where(lax.rem(turn, 2) == 1, z + away, z - away), planes)
+
+    to_sibling = pltpu.make_async_remote_copy(
+        p2_send.at[pl.ds(pl.multiple_of((1 - core) * half * WINDOW, 8), half * WINDOW)],
+        p2_sib, sib_ss, sib_rs, device_id=(sibling, col), device_id_type=MESH,
+    )
+    to_sibling.start()
+    to_sibling.wait()
+    mine_first = core == 0
+
+    @pl.loop(0, half)
+    def _(u):
+        first, second = [], []
+        for g in range(4):
+            mine = p2_send[pl.ds(pl.multiple_of((core * half + u) * WINDOW + 8 * g, 8), 8), :]
+            other = p2_sib[pl.ds(pl.multiple_of(u * WINDOW + 8 * g, 8), 8), :]
+            first.append(jnp.where(mine_first, mine, other))
+            second.append(jnp.where(mine_first, other, mine))
+        total = [first[0]] + [first[g] + second[g - 1] for g in range(1, 4)] + [second[3]]
+        p2_chip[pl.ds(pl.multiple_of(u * WIDE, 8), WIDE), :] = jnp.concatenate(total, axis=0)
+
+    is_owner, row_me = place(z, x)
+
+    @pl.loop(0, planes)
+    def _(turn):
+        zt = plane(turn)
+        for xt in range(2):
+            owns, u = place(zt, xt)
+            target = 4 * zt + 2 * xt + core
+
+            @pl.when(owns & (target != me))
+            def _():
+                pltpu.make_async_remote_copy(
+                    p2_chip.at[pl.ds(pl.multiple_of(u * WIDE, 8), WIDE)],
+                    p2_recv.at[pl.ds(pl.multiple_of(chip * WIDE, 8), WIDE)],
+                    p2_ss, p2_rs, device_id=(target, col), device_id_type=MESH,
+                ).start()
 
     def wait(ref, blocks, sem):
-        part = ref.at[pl.ds(0, blocks * size)]
+        part = ref.at[pl.ds(0, blocks * WIDE)]
         pltpu.make_async_copy(part, part, sem).wait()
+
+    chips = n_acq // 2
+    row_at = pl.multiple_of((core * half + row_me) * WIDE, 8)
 
     @pl.when(is_owner)
     def _():
-        p2_recv[pl.ds(pl.multiple_of(me * size, 8), size), :] = p2_send[
-            pl.ds(pl.multiple_of(row_me * size, 8), size), :
+        inverse[...] = ungrounded(eliminate(inverse[...], 8))
+        p2_recv[pl.ds(pl.multiple_of(chip * WIDE, 8), WIDE), :] = p2_chip[
+            pl.ds(pl.multiple_of(row_me * WIDE, 8), WIDE), :
         ]
-        wait(p2_recv, n_acq - 1, p2_rs)
-        sums = []
-        for m in range(2):
-
-            def part(a, h):
-                at = a * size + m * BAND + 8 * h
-                return p2_recv[at : at + 8, :]
-
-            odd[m, 0:8, :] = jnp.zeros((8, COLS), F32)
-            for v in range(16):
-                value = part(2 * v + 1, 0)
-                if v:
-                    value = value + part(2 * v - 1, 1)
-                odd[m, 8 * v + 8 : 8 * v + 16, :] = value
-            even = []
-            for v in range(16):
-                value = part(2 * v, 0)
-                if v:
-                    value = value + part(2 * v - 2, 1)
-                even.append(value)
-            sums.append(jnp.concatenate(even, axis=0) + odd[m, 4 : 4 + 128, :])
+        wait(p2_recv, chips - 1, p2_rs)
+        groups = []
+        for b in range(n_acq):
+            total = None
+            for g in range(b % 2, 5, 2):
+                c = (b - g) // 2
+                if c >= 0:
+                    part = p2_recv[c * WIDE + 8 * g : c * WIDE + 8 * g + 8, :]
+                    total = part if total is None else total + part
+            groups.append(total)
+        low = iota((8, COLS), 0) < 4
+        first, second = [], []
+        for v in range(n_acq // 2):
+            one, two = groups[2 * v], groups[2 * v + 1]
+            first.append(jnp.where(low, one, pltpu.roll(two, 4, axis=0)))
+            second.append(jnp.where(low, pltpu.roll(one, 4, axis=0), two))
+        sums = jnp.concatenate(
+            [jnp.concatenate(first, axis=0), jnp.concatenate(second, axis=0)], axis=1
+        )
         solved = jnp.dot(
-            inverse[...], jnp.concatenate(sums, axis=1),
-            precision=lax.Precision.HIGHEST, preferred_element_type=F32,
+            inverse[...], sums, precision=lax.Precision.HIGHEST, preferred_element_type=F32
         )
-        for m in range(2):
-            sol[m, 0:128, :] = solved[:, m * COLS : (m + 1) * COLS]
-            sol[m, 128:144, :] = jnp.zeros((16, COLS), F32)
-        for a in range(32):
-            for m in range(2):
-                at = a * size + m * BAND
-                p3_send[at : at + BAND, :] = sol[m, 4 * a : 4 * a + BAND, :]
-
-        @pl.loop(1, n_acq)
-        def _(i):
-            target = rem(me + i, n_acq)
-            pltpu.make_async_remote_copy(
-                p3_send.at[pl.ds(pl.multiple_of(target * size, 8), size)],
-                p3_recv.at[pl.ds(pl.multiple_of(row_me * size, 8), size)],
-                p3_ss, p3_rs, device_id=(target, col), device_id_type=MESH,
-            ).start()
-
-        p3_recv[pl.ds(pl.multiple_of(row_me * size, 8), size), :] = p3_send[
-            pl.ds(pl.multiple_of(me * size, 8), size), :
-        ]
-        wait(p2_send, ROWS - 1, p2_ss)
-        wait(p3_recv, ROWS - 1, p3_rs)
-        wait(p3_send, n_acq - 1, p3_ss)
+        for v in range(n_acq // 2):
+            one, two = solved[8 * v : 8 * v + 8, :COLS], solved[8 * v : 8 * v + 8, COLS:]
+            sol[16 * v : 16 * v + 8, :] = jnp.where(low, one, pltpu.roll(two, 4, axis=0))
+            sol[16 * v + 8 : 16 * v + 16, :] = jnp.where(low, pltpu.roll(one, 4, axis=0), two)
+        sol[8 * n_acq :, :] = jnp.zeros((24, COLS), F32)
+
+        @pl.loop(0, planes)
+        def _(turn):
+            zt = plane(turn)
+            for xt in range(2):
+                target = 4 * zt + 2 * xt + core
+
+                @pl.when(target != me)
+                def _():
+                    pltpu.make_async_remote_copy(
+                        sol.at[pl.ds(pl.multiple_of((2 * zt + xt) * 16, 8), WIDE)],
+                        p3_recv.at[pl.ds(row_at, WIDE)],
+                        p3_ss, p3_rs, device_id=(target, col), device_id_type=MESH,
+                    ).start()
+
+        p3_recv[pl.ds(row_at, WIDE), :] = sol[pl.ds(pl.multiple_of(chip * 16, 8), WIDE), :]
+        wait(p3_recv, half - 1, p3_rs)
 
     @pl.when(jnp.logical_not(is_owner))
     def _():
-        wait(p2_send, ROWS, p2_ss)
-        wait(p3_recv, ROWS, p3_rs)
+        wait(p3_recv, half, p3_rs)
+
+    own_half = pl.ds(pl.multiple_of(core * half * WIDE, 8), half * WIDE)
+    forward = pltpu.make_async_remote_copy(
+        p3_recv.at[own_half], p3_recv.at[own_half], fw_ss, fw_rs,
+        device_id=(sibling, col), device_id_type=MESH,
+    )
+    forward.start()
+
+    @pl.when(is_owner)
+    def _():
+        wait(p2_chip, half - 1, p2_ss)
+        wait(p2_recv, chips - 1, p3_ss)
+
+    @pl.when(jnp.logical_not(is_owner))
+    def _():
+        wait(p2_chip, half, p2_ss)
+
+    forward.wait()
 
     for m in range(2):
         for j in range(BAND):
-            rhs[m, j] = p3_recv[pl.ds(BAND * m + j, ROWS, stride=2 * BAND), :]
+            rhs[m, j] = p3_recv[pl.ds(8 * core + 8 * (j // 4) + 4 * m + j % 4, ROWS, stride=WIDE), :]
     for e in range(LOCAL):
         for m in range(2):
             disp_ref[e, m] = rhs[m, e]
@@ -338,7 +397,7 @@
     @pl.loop(0, LAGS)
     def _(k):
         for e in range(LOCAL):
-            live = jnp.where(live_smem[LOCAL * me + e, k] > 0, 1.0, 0.0)
+            live = jnp.where(live_smem[k, LOCAL * me + e] > 0, 1.0, 0.0)
             for m in range(2):
                 res_ref[e, k, m] = obs[e, k, m] - (rhs[m, e + k + 1] - rhs[m, e]) * live
 
@@ -353,7 +412,7 @@
             jax.ShapeDtypeStruct((LOCAL, LAGS, 2, ROWS, COLS), F32),
         ),
         in_specs=[
-            pl.BlockSpec(memory_space=pl.ANY),
+            pl.BlockSpec(memory_space=pltpu.HBM),
             pl.BlockSpec(memory_space=pltpu.VMEM),
             pl.BlockSpec(memory_space=pltpu.SMEM),
         ],
@@ -372,26 +431,22 @@
             vmem((LOCAL, LAGS, 2, ROWS, COLS), F32),
             vmem((2, BAND, ROWS, COLS), F32),
             vmem((128, 128), F32),
-            vmem((ROWS * 2 * BAND, COLS), F32),
-            vmem((n_acq * 2 * BAND, COLS), F32),
-            vmem((2, 136, COLS), F32),
-            vmem((2, 144, COLS), F32),
-            vmem((n_acq * 2 * BAND, COLS), F32),
-            vmem((ROWS * 2 * BAND, COLS), F32),
+            vmem((ROWS * WINDOW, COLS), F32),
+            vmem((ROWS // 2 * WINDOW, COLS), F32),
+            vmem((ROWS // 2 * WIDE, COLS), F32),
+            vmem((n_acq // 2 * WIDE, COLS), F32),
+            vmem((8 * n_acq + 24, COLS), F32),
+            vmem((ROWS * WIDE, COLS), F32),
             pltpu.SemaphoreType.DMA,
             pltpu.SemaphoreType.DMA((4,)),
             pltpu.SemaphoreType.DMA((4,)),
             pltpu.SemaphoreType.DMA((4, 2)),
             pltpu.SemaphoreType.DMA((4, 2)),
-            pltpu.SemaphoreType.DMA,
-            pltpu.SemaphoreType.DMA,
-            pltpu.SemaphoreType.DMA,
-            pltpu.SemaphoreType.DMA,
-        ],
+        ] + [pltpu.SemaphoreType.DMA] * 8,
         compiler_params=pltpu.CompilerParams(
             collective_id=0, has_side_effects=True, vmem_limit_bytes=32 * 1024 * 1024
         ),
-    )(samples, pair_live, pair_live)
+    )(samples, pair_live.T, pair_live.T)
 
 
 def solution(mesh):

time: 63.5 us -> 50.8 us (0.80)
  Pallas kernels: 59.4 us -> 46.7 us
    pallas_call x1, Pallas kernels: 59.4 us -> 46.7 us  [per_device(): pl.pallas_call(functools.partial(kernel, n_acq, n_col), out_shape=(jax.Sh...]
    unnamed x5 -> x6, local copies, waits for them, and re-layouts: 3.35 us -> 3.24 us
where the time goes in v2:
time: 50.8 us; the launch traced here: 50.6 us
  Pallas kernels  46.7 us (92%)
  local copies, waits for them, and re-layouts  3.24 us (6%)
  between operations  0.65 us (1%)
    pallas_call x1, Pallas kernels, per_device(): pl.pallas_call(functools.partial(kernel, n_acq, n_col), out_shape=(jax.Sh...  46.7 us
    unnamed x6, local copies, waits for them, and re-layouts  3.24 us

profile of v2, /device:TPU:1, one launch (start us, length us, event | category | flops | bytes accessed | tf_op | source)
XLA Modules:
  0.0 50.6 jit_solution(2516774855424906892)
XLA Ops:
  0.6 0.0 copy-start
  0.6 0.9 %copy-done = f32[4,2,24,128]{3,2,1,0:T(8,128)S(1)} copy-done((f32[4,2,24,128]{3,2,1,0:T(8,128)S(1)}, f32[4,2,24,128]{3,2,1,0:T(8,128)}, u32[]{:S(2)}) %copy-start) | copy-done | bytes 98328
  1.5 0.0 copy-start.1
  1.5 0.7 %copy-done.1 = s32[128,12]{0,1:T(8,128)S(1)} copy-done((s32[128,12]{0,1:T(8,128)S(1)}, s32[128,12]{0,1:T(8,128)}, u32[]{:S(2)}) %copy-start.1) | copy-done | bytes 6168
  2.2 46.7 %shard_map.41 = (f32[4,2,24,128]{3,2,1,0:T(8,128)S(1)}, f32[4,12,2,24,128]{4,3,2,1,0:T(8,128)S(1)}) custom-call(f32[4,2,24,128]{3,2,1,0:T(8,128)S(1)} %copy-done, s32[12,128]{1,0:T(8,128)S(1)} %bitcast.1, s32[12,128]{1,0:T(8,128)S(1)} %bitcast.2), custom_call_target="tpu_custom_call" | custom-call | tf_op jit(solution)/shard_map/pallas_call | solution.py:408
  48.9 0.6 %copy.6 = f32[4,2,24,128]{3,2,1,0:T(8,128)} copy(f32[4,2,24,128]{3,2,1,0:T(8,128)S(1)} %get-tuple-element.4) | data formatting | bytes 196608
  49.6 1.0 %copy.7 = f32[4,12,2,24,128]{4,3,2,1,0:T(8,128)} copy(f32[4,12,2,24,128]{4,3,2,1,0:T(8,128)S(1)} %get-tuple-element.5) | data formatting | bytes 2359296
Async XLA Ops:
  0.6 0.9 %copy-start = (f32[4,2,24,128]{3,2,1,0:T(8,128)S(1)}, f32[4,2,24,128]{3,2,1,0:T(8,128)}, u32[]{:S(2)}) copy-start(f32[4,2,24,128]{3,2,1,0:T(8,128)} %x_ref.1) | copy-start | bytes 294916
  1.5 0.7 %copy-start.1 = (s32[128,12]{0,1:T(8,128)S(1)}, s32[128,12]{0,1:T(8,128)}, u32[]{:S(2)}) copy-start(s32[128,12]{0,1:T(8,128)} %param.3) | copy-start | bytes 18436

commit v3 on v2

--- a/solution.py
+++ b/solution.py
@@ -16,7 +16,7 @@
 ROWS = 24
 COLS = 128
 GROUP = 48
-CHUNK = 384
+FIRST_GROUPS = 8
 HALO = 10
 WINDOW = 2 * BAND
 WIDE = 40
@@ -51,14 +51,15 @@
 
 def eliminate(matrix, groups):
     n = matrix.shape[0]
-    row, col = iota((n, n), 0), iota((n, n), 1)
+    lane, top = iota((1, n), 1), iota((8, n), 0)
 
     def group(_, a):
         for s in range(8):
             pivot = 1.0 / a[s : s + 1, s : s + 1]
-            scaled = jnp.where(col[:1] == s, pivot, a[s : s + 1, :] * pivot)
-            update = jnp.where(col == s, 0.0, a) - a[:, s : s + 1] * scaled
-            a = jnp.where(row == s, scaled, update)
+            hit = lane == s
+            scaled = jnp.where(hit, pivot, a[s : s + 1, :] * pivot)
+            a = jnp.where(hit, 0.0, a) - a[:, s : s + 1] * scaled
+            a = jnp.concatenate([jnp.where(top == s, scaled, a[:8]), a[8:]], axis=0)
         a = jnp.concatenate([a[8:], a[:8]], axis=0)
         return pltpu.roll(a, n - 8, axis=1)
 
@@ -85,10 +86,10 @@
 
 def kernel(
     n_acq, n_col,
-    x_ref, live_ref, live_smem, disp_ref, res_ref,
-    main, edges, packed, lhs_hi, lhs_lo, hx_hi, hx_lo, weights, ypad, scale, obs, rhs,
+    x_ref, live_hbm, disp_ref, res_ref,
+    main, edges, packed, lhs_hi, lhs_lo, weights, ypad, scale, obs, rhs,
     inverse, p2_send, p2_sib, p2_chip, p2_recv, sol, p3_recv,
-    own_sem, main_send, main_recv, edge_send, edge_recv, sib_ss, sib_rs, p2_ss, p2_rs, p3_ss, p3_rs, fw_ss, fw_rs,
+    live_ref, live_smem, own_sem, live_sem, main_send, main_recv, edge_send, edge_recv, sib_ss, sib_rs, p2_ss, p2_rs, p3_ss, p3_rs, fw_ss, fw_rs,
 ):
     me, col = lax.axis_index("acq"), lax.axis_index("col")
     left, right = rem(col - 1, n_col), rem(col + 1, n_col)
@@ -96,6 +97,12 @@
 
     own = pltpu.make_async_copy(x_ref, main.at[pl.ds(0, LOCAL)], own_sem)
     own.start()
+    lives = [
+        pltpu.make_async_copy(live_hbm, live_ref, live_sem.at[0]),
+        pltpu.make_async_copy(live_hbm, live_smem, live_sem.at[1]),
+    ]
+    for copy in lives:
+        copy.start()
 
     barrier = pltpu.get_barrier_semaphore()
 
@@ -130,9 +137,9 @@
 
     pl.semaphore_wait(barrier, 4 + n_acq // 2 - 1 + 14)
 
-    copies = []
+    blocks, sides = [], []
     for i in range(1, 4):
-        copies.append(
+        blocks.append(
             pltpu.make_async_remote_copy(
                 x_ref, main.at[pl.ds(LOCAL * i, LOCAL)], main_send.at[i], main_recv.at[i],
                 device_id=(rem(me - i, n_acq), col), device_id_type=MESH,
@@ -140,117 +147,113 @@
         )
     for i in range(4):
         for side, target in ((0, right), (1, left)):
-            copies.append(
+            sides.append(
                 pltpu.make_async_remote_copy(
                     packed.at[side], edges.at[i, side], edge_send.at[i, side], edge_recv.at[i, side],
                     device_id=(rem(me - i, n_acq), target), device_id_type=MESH,
                 )
             )
-    for copy in copies:
-        copy.start()
-
-    inverse[...] = eliminate(normal_matrix(live_ref[...]), 8)
+    for i in range(4):
+        if i:
+            blocks[i - 1].start()
+        sides[2 * i].start()
+        sides[2 * i + 1].start()
+
+    for copy in lives:
+        copy.wait()
+    inverse[...] = eliminate(normal_matrix(live_ref[...]), FIRST_GROUPS)
     weights[...] = box_weights()
     ypad[...] = jnp.zeros(ypad.shape, F32)
     rhs[...] = jnp.zeros(rhs.shape, F32)
-
-    for copy in copies:
-        copy.wait()
 
     keep_left = jnp.where(col > 0, 1.0, 0.0)
     keep_right = jnp.where(col < n_col - 1, 1.0, 0.0)
     in_left = lane < 4 * HALO
     in_right = (lane >= 4 * HALO) & (lane < 8 * HALO)
-    real, imag = [], []
-    for b in range(4):
-        low, high = edges[b, 0] * keep_left, edges[b, 1] * keep_right
-        real.append(jnp.where(in_left, low, jnp.where(in_right, pltpu.roll(high, 4 * HALO, axis=1), 0.0)))
-        imag.append(jnp.where(in_left, pltpu.roll(low, COLS - 4 * HALO, axis=1), jnp.where(in_right, high, 0.0)))
-    side_lane = jnp.where(lane >= 4 * HALO, lane - 4 * HALO, lane)
-
-    def later(parts, lag):
-        b, s = divmod(lag, 4)
-        if s == 0:
-            return parts[b]
-        return jnp.where(
-            side_lane < HALO * (4 - s),
-            pltpu.roll(parts[b], COLS - HALO * s, axis=1),
-            pltpu.roll(parts[b + 1], HALO * (4 - s), axis=1),
-        )
-
-    for k in range(LAGS):
-        later_re, later_im = later(real, k + 1), later(imag, k + 1)
-        cross = jnp.concatenate(
-            [
-                real[0] * later_re + imag[0] * later_im,
-                imag[0] * later_re - real[0] * later_im,
-            ],
-            axis=0,
-        )
-        hx_hi[k], hx_lo[k] = split(cross)
 
     def slot_of(lanes, i):
         place = jnp.where(lanes >= 4 * HALO, lanes - 4 * HALO, lanes)
         return (place >= HALO * i) & (place < HALO * (i + 1)) & (lanes < 8 * HALO)
 
+    lane_wide = iota((GROUP, COLS), 1)
+    slots = [jnp.where(slot_of(lane_wide, i), 1.0, 0.0).astype(BF16) for i in range(LOCAL)]
+
+    def turned(value, by):
+        return pltpu.roll(value, by % COLS, axis=1) if by % COLS else value
+
+    at_row = 0
     for b in range(4):
-        edge_power = real[b] * real[b] + imag[b] * imag[b]
+        if b:
+            blocks[b - 1].wait_recv()
+        sides[2 * b].wait_recv()
+        sides[2 * b + 1].wait_recv()
+        low, high = edges[b, 0] * keep_left, edges[b, 1] * keep_right
+        real = jnp.where(in_left, low, jnp.where(in_right, turned(high, 4 * HALO), 0.0))
+        imag = jnp.where(in_left, turned(low, -4 * HALO), jnp.where(in_right, high, 0.0))
+        if b == 0:
+            own_real, own_imag = real, imag
+        first_row = at_row
+        edge_power = real * real + imag * imag
         for h in range(2):
-            parts, sides = [], []
+            parts, outer = [], []
             for i in (2 * h, 2 * h + 1):
                 re, im = main[LOCAL * b + i, 0], main[LOCAL * b + i, 1]
                 parts.append(re * re + im * im)
-                sides.append(jnp.where(slot_of(lane, i), edge_power, 0.0))
-            at = pl.ds((2 * b + h) * GROUP, GROUP)
+                outer.append(jnp.where(slot_of(lane, i), edge_power, 0.0))
+            at = pl.ds(at_row, GROUP)
             lhs_hi[at, :COLS], lhs_lo[at, :COLS] = split(jnp.concatenate(parts, axis=0))
-            lhs_hi[at, COLS:], lhs_lo[at, COLS:] = split(jnp.concatenate(sides, axis=0))
-
-    lane_wide = iota((GROUP, COLS), 1)
-    slots = [jnp.where(slot_of(lane_wide, i), 1.0, 0.0).astype(BF16) for i in range(LOCAL)]
-
-    @pl.loop(0, LAGS)
-    def _(k):
-        side_hi, side_lo = hx_hi[k], hx_lo[k]
-        for e in range(LOCAL):
-            re, im = main[e, 0], main[e, 1]
-            re_j, im_j = main[e + k + 1, 0], main[e + k + 1, 1]
-            cross = jnp.concatenate([re * re_j + im * im_j, im * re_j - re * im_j], axis=0)
-            at = pl.ds(pl.multiple_of(CHUNK + k * (LOCAL * GROUP) + e * GROUP, 16), GROUP)
-            lhs_hi[at, :COLS], lhs_lo[at, :COLS] = split(cross)
-            lhs_hi[at, COLS:] = side_hi * slots[e]
-            lhs_lo[at, COLS:] = side_lo * slots[e]
-
-    def looked(chunk):
-        at = pl.ds(pl.multiple_of(chunk * CHUNK, 16), CHUNK)
+            lhs_hi[at, COLS:], lhs_lo[at, COLS:] = split(jnp.concatenate(outer, axis=0))
+            at_row += GROUP
+        pairs = []
+        for t in range(-3, 4):
+            lag = 4 * b + t
+            if not 1 <= lag <= LAGS:
+                continue
+            later_re, later_im = turned(real, -HALO * t), turned(imag, -HALO * t)
+            side_hi, side_lo = split(
+                jnp.concatenate(
+                    [
+                        own_real * later_re + own_imag * later_im,
+                        own_imag * later_re - own_real * later_im,
+                    ],
+                    axis=0,
+                )
+            )
+            for e in range(max(0, -t), min(LOCAL, LOCAL - t)):
+                re, im = main[e, 0], main[e, 1]
+                re_j, im_j = main[e + lag, 0], main[e + lag, 1]
+                cross = jnp.concatenate([re * re_j + im * im_j, im * re_j - re * im_j], axis=0)
+                at = pl.ds(at_row, GROUP)
+                lhs_hi[at, :COLS], lhs_lo[at, :COLS] = split(cross)
+                lhs_hi[at, COLS:] = side_hi * slots[e]
+                lhs_lo[at, COLS:] = side_lo * slots[e]
+                at_row += GROUP
+                pairs.append((e, lag))
+
+        at = pl.ds(first_row, at_row - first_row)
         by_cols = jnp.dot(lhs_hi[at, :], weights[...], preferred_element_type=F32)
         by_cols = by_cols + jnp.dot(lhs_lo[at, :], weights[...], preferred_element_type=F32)
-        ypad[:, 8 : 8 + ROWS, :] = by_cols.reshape(CHUNK // ROWS, ROWS, COLS)
-
-        def one(i):
+        first, count = first_row // ROWS, (at_row - first_row) // ROWS
+        ypad[pl.ds(first, count), 8 : 8 + ROWS, :] = by_cols.reshape(count, ROWS, COLS)
+
+        def looked(i):
             total = ypad[i, 6 : 6 + ROWS, :]
-            for t in range(1, 5):
-                total = total + ypad[i, 6 + t : 6 + t + ROWS, :]
+            for step in range(1, 5):
+                total = total + ypad[i, 6 + step : 6 + step + ROWS, :]
             return total
 
-        return one
-
-    power = looked(0)
-    for i in range(BAND):
-        scale[i] = lax.rsqrt(power(i))
-
-    @pl.loop(1, LAGS // 2 + 1)
-    def _(chunk):
-        one = looked(chunk)
-        for half in range(2):
-            k = 2 * chunk - 2 + half
-            for e in range(LOCAL):
-                live = jnp.where(live_smem[k, LOCAL * me + e] > 0, 1.0, 0.0)
-                factor = scale[e] * scale[e + k + 1] * live
-                for m in range(2):
-                    value = one((half * LOCAL + e) * 2 + m) * factor
-                    obs[e, k, m] = value
-                    rhs[m, e] = rhs[m, e] - value
-                    rhs[m, e + k + 1] = rhs[m, e + k + 1] + value
+        for i in range(LOCAL):
+            scale[LOCAL * b + i] = lax.rsqrt(looked(first + i))
+        for place, (e, lag) in enumerate(pairs):
+            live = jnp.where(live_smem[lag - 1, LOCAL * me + e] > 0, 1.0, 0.0)
+            factor = scale[e] * scale[e + lag] * live
+            for m in range(2):
+                value = looked(first + LOCAL + 2 * place + m) * factor
+                obs[e, lag - 1, m] = value
+                rhs[m, e] = rhs[m, e] - value
+                rhs[m, e + lag] = rhs[m, e + lag] + value
+    for copy in blocks + sides:
+        copy.wait_send()
 
     for m in range(2):
         for j in range(BAND):
@@ -316,7 +319,7 @@
 
     @pl.when(is_owner)
     def _():
-        inverse[...] = ungrounded(eliminate(inverse[...], 8))
+        inverse[...] = ungrounded(eliminate(inverse[...], 16 - FIRST_GROUPS))
         p2_recv[pl.ds(pl.multiple_of(chip * WIDE, 8), WIDE), :] = p2_chip[
             pl.ds(pl.multiple_of(row_me * WIDE, 8), WIDE), :
         ]
@@ -350,7 +353,7 @@
 
         @pl.loop(0, planes)
         def _(turn):
-            zt = plane(turn)
+            zt = turn
             for xt in range(2):
                 target = 4 * zt + 2 * xt + core
 
@@ -404,7 +407,7 @@
 
 def per_device(n_acq, n_col, samples, pair_live):
     vmem = pltpu.VMEM
-    rows_all = CHUNK + LAGS * LOCAL * GROUP
+    rows_all = BAND * ROWS + LAGS * LOCAL * GROUP
     return pl.pallas_call(
         functools.partial(kernel, n_acq, n_col),
         out_shape=(
@@ -413,8 +416,7 @@
         ),
         in_specs=[
             pl.BlockSpec(memory_space=pltpu.HBM),
-            pl.BlockSpec(memory_space=pltpu.VMEM),
-            pl.BlockSpec(memory_space=pltpu.SMEM),
+            pl.BlockSpec(memory_space=pltpu.HBM),
         ],
         out_specs=(pl.BlockSpec(memory_space=pltpu.VMEM), pl.BlockSpec(memory_space=pltpu.VMEM)),
         scratch_shapes=[
@@ -423,10 +425,8 @@
             vmem((2, ROWS, COLS), F32),
             vmem((rows_all, 2 * COLS), BF16),
             vmem((rows_all, 2 * COLS), BF16),
-            vmem((LAGS, GROUP, COLS), BF16),
-            vmem((LAGS, GROUP, COLS), BF16),
             vmem((2 * COLS, COLS), BF16),
-            vmem((CHUNK // ROWS, 40, COLS), F32),
+            vmem((rows_all // ROWS, 40, COLS), F32),
             vmem((BAND, ROWS, COLS), F32),
             vmem((LOCAL, LAGS, 2, ROWS, COLS), F32),
             vmem((2, BAND, ROWS, COLS), F32),
@@ -437,7 +437,10 @@
             vmem((n_acq // 2 * WIDE, COLS), F32),
             vmem((8 * n_acq + 24, COLS), F32),
             vmem((ROWS * WIDE, COLS), F32),
+            vmem((LAGS, 4 * n_acq), jnp.int32),
+            pltpu.SMEM((LAGS, 4 * n_acq), jnp.int32),
             pltpu.SemaphoreType.DMA,
+            pltpu.SemaphoreType.DMA((2,)),
             pltpu.SemaphoreType.DMA((4,)),
             pltpu.SemaphoreType.DMA((4,)),
             pltpu.SemaphoreType.DMA((4, 2)),
@@ -446,7 +449,7 @@
         compiler_params=pltpu.CompilerParams(
             collective_id=0, has_side_effects=True, vmem_limit_bytes=32 * 1024 * 1024
         ),
-    )(samples, pair_live.T, pair_live.T)
+    )(samples, pair_live.T)
 
 
 def solution(mesh):

time: 50.8 us -> 46.6 us (0.917)
  Pallas kernels: 46.7 us -> 42.5 us
    pallas_call x1, Pallas kernels: 46.7 us -> 42.5 us  [per_device(): pl.pallas_call(functools.partial(kernel, n_acq, n_col), out_shape=(jax.Sh...]
where the time goes in v3:
time: 46.6 us; the launch traced here: 46.4 us
  Pallas kernels  42.5 us (91%)
  local copies, waits for them, and re-layouts  3.24 us (7%)
  between operations  0.65 us (1%)
    pallas_call x1, Pallas kernels, per_device(): pl.pallas_call(functools.partial(kernel, n_acq, n_col), out_shape=(jax.Sh...  42.5 us
    unnamed x6, local copies, waits for them, and re-layouts  3.24 us

profile of v3, /device:TPU:1, one launch (start us, length us, event | category | flops | bytes accessed | tf_op | source)
XLA Modules:
  0.0 46.4 jit_solution(5635458977543593367)
XLA Ops:
  0.6 0.0 copy-start
  0.6 0.9 %copy-done = f32[4,2,24,128]{3,2,1,0:T(8,128)S(1)} copy-done((f32[4,2,24,128]{3,2,1,0:T(8,128)S(1)}, f32[4,2,24,128]{3,2,1,0:T(8,128)}, u32[]{:S(2)}) %copy-start) | copy-done | bytes 98328
  1.5 0.0 copy-start.1
  1.5 0.7 %copy-done.1 = s32[128,12]{0,1:T(8,128)S(1)} copy-done((s32[128,12]{0,1:T(8,128)S(1)}, s32[128,12]{0,1:T(8,128)}, u32[]{:S(2)}) %copy-start.1) | copy-done | bytes 6168
  2.2 42.5 %shard_map.41 = (f32[4,2,24,128]{3,2,1,0:T(8,128)S(1)}, f32[4,12,2,24,128]{4,3,2,1,0:T(8,128)S(1)}) custom-call(f32[4,2,24,128]{3,2,1,0:T(8,128)S(1)} %copy-done, s32[12,128]{1,0:T(8,128)S(1)} %bitcast.1), custom_call_target="tpu_custom_call" | custom-call | tf_op jit(solution)/shard_map/pallas_call | solution.py:411
  44.7 0.6 %copy.6 = f32[4,2,24,128]{3,2,1,0:T(8,128)} copy(f32[4,2,24,128]{3,2,1,0:T(8,128)S(1)} %get-tuple-element.4) | data formatting | bytes 196608
  45.4 1.0 %copy.7 = f32[4,12,2,24,128]{4,3,2,1,0:T(8,128)} copy(f32[4,12,2,24,128]{4,3,2,1,0:T(8,128)S(1)} %get-tuple-element.5) | data formatting | bytes 2359296
Async XLA Ops:
  0.6 0.9 %copy-start = (f32[4,2,24,128]{3,2,1,0:T(8,128)S(1)}, f32[4,2,24,128]{3,2,1,0:T(8,128)}, u32[]{:S(2)}) copy-start(f32[4,2,24,128]{3,2,1,0:T(8,128)} %x_ref.1) | copy-start | bytes 294916
  1.5 0.7 %copy-start.1 = (s32[128,12]{0,1:T(8,128)S(1)}, s32[128,12]{0,1:T(8,128)}, u32[]{:S(2)}) copy-start(s32[128,12]{0,1:T(8,128)} %param.3) | copy-start | bytes 18436

commit v4 on v3

--- a/solution.py
+++ b/solution.py
@@ -11,15 +11,17 @@
 F32 = jnp.float32
 BF16 = jnp.bfloat16
 LOCAL = 4
-BAND = 16
+PAIR = 8
+CHAIN = 20
 LAGS = 12
 ROWS = 24
+HALF = 12
+PART = 16
 COLS = 128
-GROUP = 48
-FIRST_GROUPS = 8
+GROUP = 32
 HALO = 10
-WINDOW = 2 * BAND
 WIDE = 40
+FIRST_GROUPS = 5
 
 
 def rem(a, n):
@@ -87,16 +89,18 @@
 def kernel(
     n_acq, n_col,
     x_ref, live_hbm, disp_ref, res_ref,
-    main, edges, packed, lhs_hi, lhs_lo, weights, ypad, scale, obs, rhs,
-    inverse, p2_send, p2_sib, p2_chip, p2_recv, sol, p3_recv,
-    live_ref, live_smem, own_sem, live_sem, main_send, main_recv, edge_send, edge_recv, sib_ss, sib_rs, p2_ss, p2_rs, p3_ss, p3_rs, fw_ss, fw_rs,
+    main, edges, packed, lhs_hi, lhs_lo, weights, ypad, scale, obs, obs_in, rhs, disp,
+    inverse, p2_chip, p2_recv, sol, p3_recv,
+    live_ref, live_smem, live_sem, main_send, main_recv, edge_send, edge_recv,
+    obs_ss, obs_rs, p2_ss, p2_rs, p3_ss, p3_rs, fw_ss, fw_rs,
 ):
     me, col = lax.axis_index("acq"), lax.axis_index("col")
     left, right = rem(col - 1, n_col), rem(col + 1, n_col)
+    core, chip = lax.rem(me, 2), me // 2
+    chips = n_acq // 2
+    sibling = me + 1 - 2 * core
     lane = iota((ROWS, COLS), 1)
 
-    own = pltpu.make_async_copy(x_ref, main.at[pl.ds(0, LOCAL)], own_sem)
-    own.start()
     lives = [
         pltpu.make_async_copy(live_hbm, live_ref, live_sem.at[0]),
         pltpu.make_async_copy(live_hbm, live_smem, live_sem.at[1]),
@@ -106,58 +110,83 @@
 
     barrier = pltpu.get_barrier_semaphore()
 
-    def greet(target):
-        pl.semaphore_signal(barrier, inc=1, device_id=(target, col), device_id_type=MESH)
-
-    for i in (1, -1, 3, -3):
-        greet(rem(me + i, n_acq))
-
-    @pl.loop(1, n_acq // 2)
+    def greet(target, where):
+        pl.semaphore_signal(barrier, inc=1, device_id=(target, where), device_id_type=MESH)
+
+    greet(sibling, col)
+
+    @pl.loop(1, chips)
     def _(i):
-        greet(rem(me + 2 * i, n_acq))
-
+        greet(2 * rem(chip + i, chips) + core, col)
+
+    for i in (-2, -1, 1, 2):
+        greet(2 * rem(chip + i, chips) + 1 - core, col)
     for side in (left, right):
 
-        @pl.loop(-3, 4)
+        @pl.loop(-2, 3)
         def _(i):
-            pl.semaphore_signal(barrier, inc=1, device_id=(rem(me + i, n_acq), side), device_id_type=MESH)
-
-    own.wait()
+            greet(2 * rem(chip + i, chips), side)
+            greet(2 * rem(chip + i, chips) + 1, side)
+
     to_right = jnp.zeros((ROWS, COLS), F32)
     to_left = jnp.zeros((ROWS, COLS), F32)
     for m in range(2):
         for i in range(LOCAL):
             base = 4 * HALO * m + HALO * i
             hit = (lane >= base) & (lane < base + HALO)
-            value = main[i, m]
+            value = x_ref[i, m]
             to_right = jnp.where(hit, pltpu.roll(value, (base + HALO) % COLS, axis=1), to_right)
             to_left = jnp.where(hit, pltpu.roll(value, base, axis=1) if base else value, to_left)
     packed[0] = to_right
     packed[1] = to_left
 
-    pl.semaphore_wait(barrier, 4 + n_acq // 2 - 1 + 14)
-
-    blocks, sides = [], []
-    for i in range(1, 4):
-        blocks.append(
-            pltpu.make_async_remote_copy(
-                x_ref, main.at[pl.ds(LOCAL * i, LOCAL)], main_send.at[i], main_recv.at[i],
-                device_id=(rem(me - i, n_acq), col), device_id_type=MESH,
-            )
+    pl.semaphore_wait(barrier, chips + 4 + 20)
+
+    def window(of_core):
+        return pl.ds(pl.multiple_of(8 * of_core, 8), PART)
+
+    def block(index):
+        return main.at[pl.ds(LOCAL * index, LOCAL)]
+
+    own = pltpu.make_async_copy(x_ref.at[:, :, window(core)], block(core), main_recv.at[core])
+    own.start()
+    sends, late_sends = [], []
+
+    def send_block(number, target, of_core, index):
+        return pltpu.make_async_remote_copy(
+            x_ref.at[:, :, window(of_core)], block(index), main_send.at[number], main_recv.at[index],
+            device_id=(target, col), device_id_type=MESH,
         )
-    for i in range(4):
-        for side, target in ((0, right), (1, left)):
-            sides.append(
-                pltpu.make_async_remote_copy(
-                    packed.at[side], edges.at[i, side], edge_send.at[i, side], edge_recv.at[i, side],
-                    device_id=(rem(me - i, n_acq), target), device_id_type=MESH,
-                )
-            )
-    for i in range(4):
-        if i:
-            blocks[i - 1].start()
-        sides[2 * i].start()
-        sides[2 * i + 1].start()
+
+    def send_edge(number, target, of_core, index, side):
+        return pltpu.make_async_remote_copy(
+            packed.at[side, window(of_core)], edges.at[index, side],
+            edge_send.at[number, side], edge_recv.at[index, side],
+            device_id=(target, (right, left)[side]), device_id_type=MESH,
+        )
+
+    for side in range(2):
+        for to in range(2):
+            sends.append(send_edge(to, 2 * chip + to, to, core, side))
+    sends.append(send_block(0, sibling, 1 - core, core))
+    earlier = 2 * rem(chip - 1, chips)
+    for to in range(2):
+        sends.append(send_block(1 + to, earlier + to, to, 2 + core))
+    for to in range(2):
+        for side in range(2):
+            sends.append(send_edge(2 + to, earlier + to, to, 2 + core, side))
+    earlier = 2 * rem(chip - 2, chips)
+    for to in range(2):
+        late_sends.append(send_block(3 + to, earlier + to, to, 4))
+        for side in range(2):
+            late_sends.append(send_edge(4 + to, earlier + to, to, 4, side))
+    for copy in sends:
+        copy.start()
+
+    @pl.when(core == 0)
+    def _():
+        for copy in late_sends:
+            copy.start()
 
     for copy in lives:
         copy.wait()
@@ -168,6 +197,7 @@
 
     keep_left = jnp.where(col > 0, 1.0, 0.0)
     keep_right = jnp.where(col < n_col - 1, 1.0, 0.0)
+    lane = iota((PART, COLS), 1)
     in_left = lane < 4 * HALO
     in_right = (lane >= 4 * HALO) & (lane < 8 * HALO)
 
@@ -182,16 +212,17 @@
         return pltpu.roll(value, by % COLS, axis=1) if by % COLS else value
 
     at_row = 0
-    for b in range(4):
-        if b:
-            blocks[b - 1].wait_recv()
-        sides[2 * b].wait_recv()
-        sides[2 * b + 1].wait_recv()
+    own_real, own_imag = [], []
+    for b in range(5):
+        pltpu.make_async_copy(block(b), block(b), main_recv.at[b]).wait()
+        for side in range(2):
+            pltpu.make_async_copy(edges.at[b, side], edges.at[b, side], edge_recv.at[b, side]).wait()
         low, high = edges[b, 0] * keep_left, edges[b, 1] * keep_right
         real = jnp.where(in_left, low, jnp.where(in_right, turned(high, 4 * HALO), 0.0))
         imag = jnp.where(in_left, turned(low, -4 * HALO), jnp.where(in_right, high, 0.0))
-        if b == 0:
-            own_real, own_imag = real, imag
+        if b < 2:
+            own_real.append(real)
+            own_imag.append(imag)
         first_row = at_row
         edge_power = real * real + imag * imag
         for h in range(2):
@@ -205,66 +236,63 @@
             lhs_hi[at, COLS:], lhs_lo[at, COLS:] = split(jnp.concatenate(outer, axis=0))
             at_row += GROUP
         pairs = []
-        for t in range(-3, 4):
-            lag = 4 * b + t
+        for q, t in [(q, t) for q in range(min(b + 1, 2)) for t in range(-3, 4)]:
+            lag = 4 * (b - q) + t
             if not 1 <= lag <= LAGS:
                 continue
             later_re, later_im = turned(real, -HALO * t), turned(imag, -HALO * t)
             side_hi, side_lo = split(
                 jnp.concatenate(
                     [
-                        own_real * later_re + own_imag * later_im,
-                        own_imag * later_re - own_real * later_im,
+                        own_real[q] * later_re + own_imag[q] * later_im,
+                        own_imag[q] * later_re - own_real[q] * later_im,
                     ],
                     axis=0,
                 )
             )
-            for e in range(max(0, -t), min(LOCAL, LOCAL - t)):
+            for i in range(max(0, -t), min(LOCAL, LOCAL - t)):
+                e = LOCAL * q + i
                 re, im = main[e, 0], main[e, 1]
                 re_j, im_j = main[e + lag, 0], main[e + lag, 1]
                 cross = jnp.concatenate([re * re_j + im * im_j, im * re_j - re * im_j], axis=0)
                 at = pl.ds(at_row, GROUP)
                 lhs_hi[at, :COLS], lhs_lo[at, :COLS] = split(cross)
-                lhs_hi[at, COLS:] = side_hi * slots[e]
-                lhs_lo[at, COLS:] = side_lo * slots[e]
+                lhs_hi[at, COLS:] = side_hi * slots[i]
+                lhs_lo[at, COLS:] = side_lo * slots[i]
                 at_row += GROUP
                 pairs.append((e, lag))
 
         at = pl.ds(first_row, at_row - first_row)
         by_cols = jnp.dot(lhs_hi[at, :], weights[...], preferred_element_type=F32)
         by_cols = by_cols + jnp.dot(lhs_lo[at, :], weights[...], preferred_element_type=F32)
-        first, count = first_row // ROWS, (at_row - first_row) // ROWS
-        ypad[pl.ds(first, count), 8 : 8 + ROWS, :] = by_cols.reshape(count, ROWS, COLS)
+        first, count = first_row // PART, (at_row - first_row) // PART
+        ypad[pl.ds(first, count), 8 : 8 + PART, :] = by_cols.reshape(count, PART, COLS)
 
         def looked(i):
-            total = ypad[i, 6 : 6 + ROWS, :]
+            total = ypad[i, 6 : 6 + PART, :]
             for step in range(1, 5):
-                total = total + ypad[i, 6 + step : 6 + step + ROWS, :]
+                total = total + ypad[i, 6 + step : 6 + step + PART, :]
             return total
 
         for i in range(LOCAL):
             scale[LOCAL * b + i] = lax.rsqrt(looked(first + i))
         for place, (e, lag) in enumerate(pairs):
-            live = jnp.where(live_smem[lag - 1, LOCAL * me + e] > 0, 1.0, 0.0)
+            live = jnp.where(live_smem[lag - 1, PAIR * chip + e] > 0, 1.0, 0.0)
             factor = scale[e] * scale[e + lag] * live
             for m in range(2):
                 value = looked(first + LOCAL + 2 * place + m) * factor
-                obs[e, lag - 1, m] = value
+                obs[e // LOCAL, e % LOCAL, lag - 1, m] = value
                 rhs[m, e] = rhs[m, e] - value
                 rhs[m, e + lag] = rhs[m, e + lag] + value
-    for copy in blocks + sides:
-        copy.wait_send()
 
     for m in range(2):
-        for j in range(BAND):
-            p2_send[pl.ds(8 * (j // 4) + 4 * m + j % 4, ROWS, stride=WINDOW), :] = rhs[m, j]
-
-    core = lax.rem(me, 2)
-    chip = me // 2
+        for j in range(CHAIN):
+            p2_chip[pl.ds(8 * (j // 4) + 4 * m + j % 4, PART, stride=WIDE), :] = rhs[m, j]
+
     z, x = chip // 2, lax.rem(chip, 2)
-    sibling = me + 1 - 2 * core
     planes = n_acq // 4
-    half = ROWS // 2
+    half = HALF
+    skip = 4 * core
 
     def place(zt, xt):
         both = lax.rem(zt, 2) == core
@@ -273,25 +301,6 @@
     def plane(turn):
         away = (planes - turn) // 2
         return rem(jnp.where(lax.rem(turn, 2) == 1, z + away, z - away), planes)
-
-    to_sibling = pltpu.make_async_remote_copy(
-        p2_send.at[pl.ds(pl.multiple_of((1 - core) * half * WINDOW, 8), half * WINDOW)],
-        p2_sib, sib_ss, sib_rs, device_id=(sibling, col), device_id_type=MESH,
-    )
-    to_sibling.start()
-    to_sibling.wait()
-    mine_first = core == 0
-
-    @pl.loop(0, half)
-    def _(u):
-        first, second = [], []
-        for g in range(4):
-            mine = p2_send[pl.ds(pl.multiple_of((core * half + u) * WINDOW + 8 * g, 8), 8), :]
-            other = p2_sib[pl.ds(pl.multiple_of(u * WINDOW + 8 * g, 8), 8), :]
-            first.append(jnp.where(mine_first, mine, other))
-            second.append(jnp.where(mine_first, other, mine))
-        total = [first[0]] + [first[g] + second[g - 1] for g in range(1, 4)] + [second[3]]
-        p2_chip[pl.ds(pl.multiple_of(u * WIDE, 8), WIDE), :] = jnp.concatenate(total, axis=0)
 
     is_owner, row_me = place(z, x)
 
@@ -305,23 +314,27 @@
             @pl.when(owns & (target != me))
             def _():
                 pltpu.make_async_remote_copy(
-                    p2_chip.at[pl.ds(pl.multiple_of(u * WIDE, 8), WIDE)],
+                    p2_chip.at[pl.ds(pl.multiple_of((u + skip) * WIDE, 8), WIDE)],
                     p2_recv.at[pl.ds(pl.multiple_of(chip * WIDE, 8), WIDE)],
                     p2_ss, p2_rs, device_id=(target, col), device_id_type=MESH,
                 ).start()
 
+    to_sibling = pltpu.make_async_remote_copy(
+        obs.at[1 - core], obs_in, obs_ss, obs_rs, device_id=(sibling, col), device_id_type=MESH
+    )
+    to_sibling.start()
+
     def wait(ref, blocks, sem):
         part = ref.at[pl.ds(0, blocks * WIDE)]
         pltpu.make_async_copy(part, part, sem).wait()
 
-    chips = n_acq // 2
     row_at = pl.multiple_of((core * half + row_me) * WIDE, 8)
 
     @pl.when(is_owner)
     def _():
         inverse[...] = ungrounded(eliminate(inverse[...], 16 - FIRST_GROUPS))
         p2_recv[pl.ds(pl.multiple_of(chip * WIDE, 8), WIDE), :] = p2_chip[
-            pl.ds(pl.multiple_of(row_me * WIDE, 8), WIDE), :
+            pl.ds(pl.multiple_of((row_me + skip) * WIDE, 8), WIDE), :
         ]
         wait(p2_recv, chips - 1, p2_rs)
         groups = []
@@ -388,26 +401,42 @@
     def _():
         wait(p2_chip, half, p2_ss)
 
+    for copy in sends:
+        copy.wait_send()
+
+    @pl.when(core == 0)
+    def _():
+        for copy in late_sends:
+            copy.wait_send()
+
+    to_sibling.wait()
     forward.wait()
 
     for m in range(2):
-        for j in range(BAND):
-            rhs[m, j] = p3_recv[pl.ds(8 * core + 8 * (j // 4) + 4 * m + j % 4, ROWS, stride=WIDE), :]
+        for j in range(16):
+            disp[m, j] = p3_recv[pl.ds(8 * core + 8 * (j // 4) + 4 * m + j % 4, ROWS, stride=WIDE), :]
     for e in range(LOCAL):
         for m in range(2):
-            disp_ref[e, m] = rhs[m, e]
+            disp_ref[e, m] = disp[m, e]
+    upper = iota((8, COLS), 0) < 4
+    on_first = core == 0
 
     @pl.loop(0, LAGS)
     def _(k):
         for e in range(LOCAL):
             live = jnp.where(live_smem[k, LOCAL * me + e] > 0, 1.0, 0.0)
             for m in range(2):
-                res_ref[e, k, m] = obs[e, k, m] - (rhs[m, e + k + 1] - rhs[m, e]) * live
+                mine, other = obs[core, e, k, m], obs_in[e, k, m]
+                low, high = jnp.where(on_first, mine, other), jnp.where(on_first, other, mine)
+                seen = jnp.concatenate(
+                    [low[:8], jnp.where(upper, low[8:], high[:8]), high[8:]], axis=0
+                )
+                res_ref[e, k, m] = seen - (disp[m, e + k + 1] - disp[m, e]) * live
 
 
 def per_device(n_acq, n_col, samples, pair_live):
     vmem = pltpu.VMEM
-    rows_all = BAND * ROWS + LAGS * LOCAL * GROUP
+    rows_all = CHAIN * PART + LAGS * PAIR * GROUP
     return pl.pallas_call(
         functools.partial(kernel, n_acq, n_col),
         out_shape=(
@@ -415,36 +444,35 @@
             jax.ShapeDtypeStruct((LOCAL, LAGS, 2, ROWS, COLS), F32),
         ),
         in_specs=[
-            pl.BlockSpec(memory_space=pltpu.HBM),
+            pl.BlockSpec(memory_space=pltpu.VMEM),
             pl.BlockSpec(memory_space=pltpu.HBM),
         ],
         out_specs=(pl.BlockSpec(memory_space=pltpu.VMEM), pl.BlockSpec(memory_space=pltpu.VMEM)),
         scratch_shapes=[
-            vmem((BAND, 2, ROWS, COLS), F32),
-            vmem((4, 2, ROWS, COLS), F32),
+            vmem((CHAIN, 2, PART, COLS), F32),
+            vmem((5, 2, PART, COLS), F32),
             vmem((2, ROWS, COLS), F32),
             vmem((rows_all, 2 * COLS), BF16),
             vmem((rows_all, 2 * COLS), BF16),
             vmem((2 * COLS, COLS), BF16),
-            vmem((rows_all // ROWS, 40, COLS), F32),
-            vmem((BAND, ROWS, COLS), F32),
-            vmem((LOCAL, LAGS, 2, ROWS, COLS), F32),
-            vmem((2, BAND, ROWS, COLS), F32),
+            vmem((rows_all // PART, 32, COLS), F32),
+            vmem((CHAIN, PART, COLS), F32),
+            vmem((2, LOCAL, LAGS, 2, PART, COLS), F32),
+            vmem((LOCAL, LAGS, 2, PART, COLS), F32),
+            vmem((2, CHAIN, PART, COLS), F32),
+            vmem((2, 16, ROWS, COLS), F32),
             vmem((128, 128), F32),
-            vmem((ROWS * WINDOW, COLS), F32),
-            vmem((ROWS // 2 * WINDOW, COLS), F32),
-            vmem((ROWS // 2 * WIDE, COLS), F32),
+            vmem((PART * WIDE, COLS), F32),
             vmem((n_acq // 2 * WIDE, COLS), F32),
             vmem((8 * n_acq + 24, COLS), F32),
             vmem((ROWS * WIDE, COLS), F32),
             vmem((LAGS, 4 * n_acq), jnp.int32),
             pltpu.SMEM((LAGS, 4 * n_acq), jnp.int32),
-            pltpu.SemaphoreType.DMA,
             pltpu.SemaphoreType.DMA((2,)),
-            pltpu.SemaphoreType.DMA((4,)),
-            pltpu.SemaphoreType.DMA((4,)),
-            pltpu.SemaphoreType.DMA((4, 2)),
-            pltpu.SemaphoreType.DMA((4, 2)),
+            pltpu.SemaphoreType.DMA((5,)),
+            pltpu.SemaphoreType.DMA((5,)),
+            pltpu.SemaphoreType.DMA((6, 2)),
+            pltpu.SemaphoreType.DMA((5, 2)),
         ] + [pltpu.SemaphoreType.DMA] * 8,
         compiler_params=pltpu.CompilerParams(
             collective_id=0, has_side_effects=True, vmem_limit_bytes=32 * 1024 * 1024

time: 46.6 us -> 45.2 us (0.970)
  Pallas kernels: 42.5 us -> 41.1 us
    pallas_call x1, Pallas kernels: 42.5 us -> 41.1 us  [per_device(): pl.pallas_call(functools.partial(kernel, n_acq, n_col), out_shape=(jax.Sh...]
where the time goes in v4:
time: 45.2 us; the launch traced here: 45 us
  Pallas kernels  41.1 us (91%)
  local copies, waits for them, and re-layouts  3.24 us (7%)
  between operations  0.65 us (1%)
    pallas_call x1, Pallas kernels, per_device(): pl.pallas_call(functools.partial(kernel, n_acq, n_col), out_shape=(jax.Sh...  41.1 us
    unnamed x6, local copies, waits for them, and re-layouts  3.24 us

profile of v4, /device:TPU:1, one launch (start us, length us, event | category | flops | bytes accessed | tf_op | source)
XLA Modules:
  0.0 45.0 jit_solution(1693857714887342887)
XLA Ops:
  0.6 0.0 copy-start
  0.6 0.9 %copy-done = f32[4,2,24,128]{3,2,1,0:T(8,128)S(1)} copy-done((f32[4,2,24,128]{3,2,1,0:T(8,128)S(1)}, f32[4,2,24,128]{3,2,1,0:T(8,128)}, u32[]{:S(2)}) %copy-start) | copy-done | bytes 98328
  1.5 0.0 copy-start.1
  1.5 0.7 %copy-done.1 = s32[128,12]{0,1:T(8,128)S(1)} copy-done((s32[128,12]{0,1:T(8,128)S(1)}, s32[128,12]{0,1:T(8,128)}, u32[]{:S(2)}) %copy-start.1) | copy-done | bytes 6168
  2.2 41.1 %shard_map.41 = (f32[4,2,24,128]{3,2,1,0:T(8,128)S(1)}, f32[4,12,2,24,128]{4,3,2,1,0:T(8,128)S(1)}) custom-call(f32[4,2,24,128]{3,2,1,0:T(8,128)S(1)} %copy-done, s32[12,128]{1,0:T(8,128)S(1)} %bitcast.1), custom_call_target="tpu_custom_call" | custom-call | tf_op jit(solution)/shard_map/pallas_call | solution.py:440
  43.4 0.6 %copy.6 = f32[4,2,24,128]{3,2,1,0:T(8,128)} copy(f32[4,2,24,128]{3,2,1,0:T(8,128)S(1)} %get-tuple-element.4) | data formatting | bytes 196608
  44.0 1.0 %copy.7 = f32[4,12,2,24,128]{4,3,2,1,0:T(8,128)} copy(f32[4,12,2,24,128]{4,3,2,1,0:T(8,128)S(1)} %get-tuple-element.5) | data formatting | bytes 2359296
Async XLA Ops:
  0.6 0.9 %copy-start = (f32[4,2,24,128]{3,2,1,0:T(8,128)S(1)}, f32[4,2,24,128]{3,2,1,0:T(8,128)}, u32[]{:S(2)}) copy-start(f32[4,2,24,128]{3,2,1,0:T(8,128)} %x_ref.1) | copy-start | bytes 294916
  1.5 0.7 %copy-start.1 = (s32[128,12]{0,1:T(8,128)S(1)}, s32[128,12]{0,1:T(8,128)}, u32[]{:S(2)}) copy-start(s32[128,12]{0,1:T(8,128)} %param.3) | copy-start | bytes 18436

commit v5 on v4

--- a/solution.py
+++ b/solution.py
@@ -88,10 +88,10 @@
 
 def kernel(
     n_acq, n_col,
-    x_ref, live_hbm, disp_ref, res_ref,
+    x_hbm, live_hbm, disp_ref, res_ref,
     main, edges, packed, lhs_hi, lhs_lo, weights, ypad, scale, obs, obs_in, rhs, disp,
     inverse, p2_chip, p2_recv, sol, p3_recv,
-    live_ref, live_smem, live_sem, main_send, main_recv, edge_send, edge_recv,
+    x_ref, live_ref, live_smem, own_sem, live_sem, main_send, main_recv, edge_send, edge_recv,
     obs_ss, obs_rs, p2_ss, p2_rs, p3_ss, p3_rs, fw_ss, fw_rs,
 ):
     me, col = lax.axis_index("acq"), lax.axis_index("col")
@@ -101,6 +101,8 @@
     sibling = me + 1 - 2 * core
     lane = iota((ROWS, COLS), 1)
 
+    fetch = pltpu.make_async_copy(x_hbm, x_ref, own_sem)
+    fetch.start()
     lives = [
         pltpu.make_async_copy(live_hbm, live_ref, live_sem.at[0]),
         pltpu.make_async_copy(live_hbm, live_smem, live_sem.at[1]),
@@ -128,6 +130,7 @@
             greet(2 * rem(chip + i, chips), side)
             greet(2 * rem(chip + i, chips) + 1, side)
 
+    fetch.wait()
     to_right = jnp.zeros((ROWS, COLS), F32)
     to_left = jnp.zeros((ROWS, COLS), F32)
     for m in range(2):
@@ -434,17 +437,27 @@
                 res_ref[e, k, m] = seen - (disp[m, e + k + 1] - disp[m, e]) * live
 
 
+def place_out(disp_in, res_in, disp_out, res_out, sems):
+    copies = [pltpu.make_async_copy(disp_in, disp_out, sems.at[LOCAL])]
+    for e in range(LOCAL):
+        copies.append(pltpu.make_async_copy(res_in.at[e], res_out.at[e], sems.at[e]))
+    for copy in copies:
+        copy.start()
+    for copy in copies:
+        copy.wait()
+
+
 def per_device(n_acq, n_col, samples, pair_live):
     vmem = pltpu.VMEM
     rows_all = CHAIN * PART + LAGS * PAIR * GROUP
-    return pl.pallas_call(
+    results = pl.pallas_call(
         functools.partial(kernel, n_acq, n_col),
         out_shape=(
             jax.ShapeDtypeStruct((LOCAL, 2, ROWS, COLS), F32),
             jax.ShapeDtypeStruct((LOCAL, LAGS, 2, ROWS, COLS), F32),
         ),
         in_specs=[
-            pl.BlockSpec(memory_space=pltpu.VMEM),
+            pl.BlockSpec(memory_space=pltpu.HBM),
             pl.BlockSpec(memory_space=pltpu.HBM),
         ],
         out_specs=(pl.BlockSpec(memory_space=pltpu.VMEM), pl.BlockSpec(memory_space=pltpu.VMEM)),
@@ -466,8 +479,10 @@
             vmem((n_acq // 2 * WIDE, COLS), F32),
             vmem((8 * n_acq + 24, COLS), F32),
             vmem((ROWS * WIDE, COLS), F32),
+            vmem((LOCAL, 2, ROWS, COLS), F32),
             vmem((LAGS, 4 * n_acq), jnp.int32),
             pltpu.SMEM((LAGS, 4 * n_acq), jnp.int32),
+            pltpu.SemaphoreType.DMA,
             pltpu.SemaphoreType.DMA((2,)),
             pltpu.SemaphoreType.DMA((5,)),
             pltpu.SemaphoreType.DMA((5,)),
@@ -477,7 +492,15 @@
         compiler_params=pltpu.CompilerParams(
             collective_id=0, has_side_effects=True, vmem_limit_bytes=32 * 1024 * 1024
         ),
-    )(samples, pair_live.T)
+    )(pltpu.with_memory_space_constraint(samples, pltpu.HBM), pltpu.with_memory_space_constraint(pair_live.T, pltpu.HBM))
+    return pl.pallas_call(
+        place_out,
+        out_shape=tuple(jax.ShapeDtypeStruct(r.shape, F32) for r in results),
+        in_specs=[pl.BlockSpec(memory_space=pl.ANY)] * 2,
+        out_specs=(pl.BlockSpec(memory_space=pl.ANY),) * 2,
+        scratch_shapes=[pltpu.SemaphoreType.DMA((LOCAL + 1,))],
+        compiler_params=pltpu.CompilerParams(vmem_limit_bytes=4 * 1024 * 1024),
+    )(*results)
 
 
 def solution(mesh):

time: 45.2 us -> 43 us (0.951)
  local copies, waits for them, and re-layouts: 3.24 us -> 0 us
  Pallas kernels: 41.1 us -> 42.3 us
    unnamed x6 -> x0, local copies, waits for them, and re-layouts: 3.24 us -> none
    pallas_call x0 -> x1, Pallas kernels: none -> 1.08 us  [per_device(): pl.pallas_call(place_out, out_shape=tuple((jax.ShapeDtypeStruct(r.shape,...]
where the time goes in v5:
time: 43 us; the launch traced here: 42.9 us
  Pallas kernels  42.3 us (98%)
  between operations  0.64 us (1%)
    pallas_call x1, Pallas kernels, per_device(): pl.pallas_call(functools.partial(kernel, n_acq, n_col), out_shape=(jax.Sh...  41.2 us
    pallas_call x1, Pallas kernels, per_device(): pl.pallas_call(place_out, out_shape=tuple((jax.ShapeDtypeStruct(r.shape,...  1.08 us

profile of v5, /device:TPU:1, one launch (start us, length us, event | category | flops | bytes accessed | tf_op | source)
XLA Modules:
  0.0 42.9 jit_solution(14421392768544109610)
XLA Ops:
  0.6 41.2 %shard_map.41 = (f32[4,2,24,128]{3,2,1,0:T(8,128)S(1)}, f32[4,12,2,24,128]{4,3,2,1,0:T(8,128)S(1)}) custom-call(f32[4,2,24,128]{3,2,1,0:T(8,128)} %x_hbm.1, s32[12,128]{1,0:T(8,128)} %bitcast.1), custom_call_target="tpu_custom_call" | custom-call | tf_op jit(solution)/shard_map/pallas_call | solution.py:453
  41.8 1.1 %shard_map.42 = (f32[4,2,24,128]{3,2,1,0:T(8,128)}, f32[4,12,2,24,128]{4,3,2,1,0:T(8,128)}) custom-call(f32[4,2,24,128]{3,2,1,0:T(8,128)S(1)} %get-tuple-element.4.disp_in, f32[4,12,2,24,128]{4,3,2,1,0:T(8,128)S(1)} %get-tuple-element.5.res_in), custom_call_target="tpu_custom_call" | custom-call | tf_op jit(solution)/shard_map/pallas_call | solution.py:496

commit v6 on v5

--- a/solution.py
+++ b/solution.py
@@ -117,7 +117,7 @@
 
     greet(sibling, col)
 
-    @pl.loop(1, chips)
+    @pl.loop(1, chips, unroll=True)
     def _(i):
         greet(2 * rem(chip + i, chips) + core, col)
 
@@ -125,7 +125,7 @@
         greet(2 * rem(chip + i, chips) + 1 - core, col)
     for side in (left, right):
 
-        @pl.loop(-2, 3)
+        @pl.loop(-2, 3, unroll=True)
         def _(i):
             greet(2 * rem(chip + i, chips), side)
             greet(2 * rem(chip + i, chips) + 1, side)
@@ -307,7 +307,7 @@
 
     is_owner, row_me = place(z, x)
 
-    @pl.loop(0, planes)
+    @pl.loop(0, planes, unroll=True)
     def _(turn):
         zt = plane(turn)
         for xt in range(2):
@@ -367,7 +367,7 @@
             sol[16 * v + 8 : 16 * v + 16, :] = jnp.where(low, pltpu.roll(one, 4, axis=0), two)
         sol[8 * n_acq :, :] = jnp.zeros((24, COLS), F32)
 
-        @pl.loop(0, planes)
+        @pl.loop(0, planes, unroll=True)
         def _(turn):
             zt = turn
             for xt in range(2):
@@ -382,6 +382,23 @@
                     ).start()
 
         p3_recv[pl.ds(row_at, WIDE), :] = sol[pl.ds(pl.multiple_of(chip * 16, 8), WIDE), :]
+
+    to_sibling.wait()
+    upper = iota((8, COLS), 0) < 4
+    on_first = core == 0
+
+    @pl.loop(0, LAGS)
+    def _(k):
+        for e in range(LOCAL):
+            for m in range(2):
+                mine, other = obs[core, e, k, m], obs_in[e, k, m]
+                low, high = jnp.where(on_first, mine, other), jnp.where(on_first, other, mine)
+                res_ref[e, k, m] = jnp.concatenate(
+                    [low[:8], jnp.where(upper, low[8:], high[:8]), high[8:]], axis=0
+                )
+
+    @pl.when(is_owner)
+    def _():
         wait(p3_recv, half - 1, p3_rs)
 
     @pl.when(jnp.logical_not(is_owner))
@@ -394,25 +411,6 @@
         device_id=(sibling, col), device_id_type=MESH,
     )
     forward.start()
-
-    @pl.when(is_owner)
-    def _():
-        wait(p2_chip, half - 1, p2_ss)
-        wait(p2_recv, chips - 1, p3_ss)
-
-    @pl.when(jnp.logical_not(is_owner))
-    def _():
-        wait(p2_chip, half, p2_ss)
-
-    for copy in sends:
-        copy.wait_send()
-
-    @pl.when(core == 0)
-    def _():
-        for copy in late_sends:
-            copy.wait_send()
-
-    to_sibling.wait()
     forward.wait()
 
     for m in range(2):
@@ -421,20 +419,30 @@
     for e in range(LOCAL):
         for m in range(2):
             disp_ref[e, m] = disp[m, e]
-    upper = iota((8, COLS), 0) < 4
-    on_first = core == 0
-
-    @pl.loop(0, LAGS)
+
+    @pl.loop(0, LAGS, unroll=3)
     def _(k):
         for e in range(LOCAL):
             live = jnp.where(live_smem[k, LOCAL * me + e] > 0, 1.0, 0.0)
             for m in range(2):
-                mine, other = obs[core, e, k, m], obs_in[e, k, m]
-                low, high = jnp.where(on_first, mine, other), jnp.where(on_first, other, mine)
-                seen = jnp.concatenate(
-                    [low[:8], jnp.where(upper, low[8:], high[:8]), high[8:]], axis=0
-                )
-                res_ref[e, k, m] = seen - (disp[m, e + k + 1] - disp[m, e]) * live
+                res_ref[e, k, m] = res_ref[e, k, m] - (disp[m, e + k + 1] - disp[m, e]) * live
+
+    @pl.when(is_owner)
+    def _():
+        wait(p2_chip, half - 1, p2_ss)
+        wait(p2_recv, chips - 1, p3_ss)
+
+    @pl.when(jnp.logical_not(is_owner))
+    def _():
+        wait(p2_chip, half, p2_ss)
+
+    for copy in sends:
+        copy.wait_send()
+
+    @pl.when(core == 0)
+    def _():
+        for copy in late_sends:
+            copy.wait_send()
 
 
 def place_out(disp_in, res_in, disp_out, res_out, sems):

time: 43 us -> 42.6 us (level)
  Pallas kernels: 42.3 us -> 41.8 us
    pallas_call x1, Pallas kernels: 41.2 us -> 40.7 us  [per_device(): pl.pallas_call(functools.partial(kernel, n_acq, n_col), out_shape=(jax.Sh...]
where the time goes in v6:
time: 42.6 us; the launch traced here: 42.4 us
  Pallas kernels  41.8 us (98%)
  between operations  0.64 us (2%)
    pallas_call x1, Pallas kernels, per_device(): pl.pallas_call(functools.partial(kernel, n_acq, n_col), out_shape=(jax.Sh...  40.7 us
    pallas_call x1, Pallas kernels, per_device(): pl.pallas_call(place_out, out_shape=tuple((jax.ShapeDtypeStruct(r.shape,...  1.08 us

profile of v6, /device:TPU:1, one launch (start us, length us, event | category | flops | bytes accessed | tf_op | source)
XLA Modules:
  0.0 42.4 jit_solution(14778163543119712073)
XLA Ops:
  0.6 40.7 %shard_map.41 = (f32[4,2,24,128]{3,2,1,0:T(8,128)S(1)}, f32[4,12,2,24,128]{4,3,2,1,0:T(8,128)S(1)}) custom-call(f32[4,2,24,128]{3,2,1,0:T(8,128)} %x_hbm.1, s32[12,128]{1,0:T(8,128)} %bitcast.1), custom_call_target="tpu_custom_call" | custom-call | tf_op jit(solution)/shard_map/pallas_call | solution.py:461
  41.3 1.1 %shard_map.42 = (f32[4,2,24,128]{3,2,1,0:T(8,128)}, f32[4,12,2,24,128]{4,3,2,1,0:T(8,128)}) custom-call(f32[4,2,24,128]{3,2,1,0:T(8,128)S(1)} %get-tuple-element.4.disp_in, f32[4,12,2,24,128]{4,3,2,1,0:T(8,128)S(1)} %get-tuple-element.5.res_in), custom_call_target="tpu_custom_call" | custom-call | tf_op jit(solution)/shard_map/pallas_call | solution.py:504

commit v7 on v6

--- a/solution.py
+++ b/solution.py
@@ -88,8 +88,8 @@
 
 def kernel(
     n_acq, n_col,
-    x_hbm, live_hbm, disp_ref, res_ref,
-    main, edges, packed, lhs_hi, lhs_lo, weights, ypad, scale, obs, obs_in, rhs, disp,
+    x_hbm, live_hbm, disp, res_ref, flags,
+    main, edges, packed, lhs_hi, lhs_lo, weights, ypad, scale, obs, obs_in, rhs,
     inverse, p2_chip, p2_recv, sol, p3_recv,
     x_ref, live_ref, live_smem, own_sem, live_sem, main_send, main_recv, edge_send, edge_recv,
     obs_ss, obs_rs, p2_ss, p2_rs, p3_ss, p3_rs, fw_ss, fw_rs,
@@ -390,6 +390,8 @@
     @pl.loop(0, LAGS)
     def _(k):
         for e in range(LOCAL):
+            live = jnp.where(live_smem[k, LOCAL * me + e] > 0, 1.0, 0.0)
+            flags[LOCAL * k + e] = jnp.full((8, COLS), live, F32)
             for m in range(2):
                 mine, other = obs[core, e, k, m], obs_in[e, k, m]
                 low, high = jnp.where(on_first, mine, other), jnp.where(on_first, other, mine)
@@ -416,41 +418,38 @@
     for m in range(2):
         for j in range(16):
             disp[m, j] = p3_recv[pl.ds(8 * core + 8 * (j // 4) + 4 * m + j % 4, ROWS, stride=WIDE), :]
+
+    @pl.when(is_owner)
+    def _():
+        wait(p2_chip, half - 1, p2_ss)
+        wait(p2_recv, chips - 1, p3_ss)
+
+    @pl.when(jnp.logical_not(is_owner))
+    def _():
+        wait(p2_chip, half, p2_ss)
+
+    for copy in sends:
+        copy.wait_send()
+
+    @pl.when(core == 0)
+    def _():
+        for copy in late_sends:
+            copy.wait_send()
+
+
+def finish(disp, seen, flags, disp_out, res_out, own, res, sems):
     for e in range(LOCAL):
         for m in range(2):
-            disp_ref[e, m] = disp[m, e]
-
-    @pl.loop(0, LAGS, unroll=3)
-    def _(k):
-        for e in range(LOCAL):
-            live = jnp.where(live_smem[k, LOCAL * me + e] > 0, 1.0, 0.0)
+            own[e, m] = disp[m, e]
+    copies = [pltpu.make_async_copy(own, disp_out, sems.at[LOCAL])]
+    copies[0].start()
+    for e in range(LOCAL):
+        for k in range(LAGS):
+            live = flags[LOCAL * k + e, 0:1, :]
             for m in range(2):
-                res_ref[e, k, m] = res_ref[e, k, m] - (disp[m, e + k + 1] - disp[m, e]) * live
-
-    @pl.when(is_owner)
-    def _():
-        wait(p2_chip, half - 1, p2_ss)
-        wait(p2_recv, chips - 1, p3_ss)
-
-    @pl.when(jnp.logical_not(is_owner))
-    def _():
-        wait(p2_chip, half, p2_ss)
-
-    for copy in sends:
-        copy.wait_send()
-
-    @pl.when(core == 0)
-    def _():
-        for copy in late_sends:
-            copy.wait_send()
-
-
-def place_out(disp_in, res_in, disp_out, res_out, sems):
-    copies = [pltpu.make_async_copy(disp_in, disp_out, sems.at[LOCAL])]
-    for e in range(LOCAL):
-        copies.append(pltpu.make_async_copy(res_in.at[e], res_out.at[e], sems.at[e]))
-    for copy in copies:
-        copy.start()
+                res[e, k, m] = seen[e, k, m] - (disp[m, e + k + 1] - disp[m, e]) * live
+        copies.append(pltpu.make_async_copy(res.at[e], res_out.at[e], sems.at[e]))
+        copies[-1].start()
     for copy in copies:
         copy.wait()
 
@@ -461,14 +460,15 @@
     results = pl.pallas_call(
         functools.partial(kernel, n_acq, n_col),
         out_shape=(
-            jax.ShapeDtypeStruct((LOCAL, 2, ROWS, COLS), F32),
+            jax.ShapeDtypeStruct((2, 16, ROWS, COLS), F32),
             jax.ShapeDtypeStruct((LOCAL, LAGS, 2, ROWS, COLS), F32),
+            jax.ShapeDtypeStruct((LOCAL * LAGS, 8, COLS), F32),
         ),
         in_specs=[
             pl.BlockSpec(memory_space=pltpu.HBM),
             pl.BlockSpec(memory_space=pltpu.HBM),
         ],
-        out_specs=(pl.BlockSpec(memory_space=pltpu.VMEM), pl.BlockSpec(memory_space=pltpu.VMEM)),
+        out_specs=(pl.BlockSpec(memory_space=pltpu.VMEM),) * 3,
         scratch_shapes=[
             vmem((CHAIN, 2, PART, COLS), F32),
             vmem((5, 2, PART, COLS), F32),
@@ -481,7 +481,6 @@
             vmem((2, LOCAL, LAGS, 2, PART, COLS), F32),
             vmem((LOCAL, LAGS, 2, PART, COLS), F32),
             vmem((2, CHAIN, PART, COLS), F32),
-            vmem((2, 16, ROWS, COLS), F32),
             vmem((128, 128), F32),
             vmem((PART * WIDE, COLS), F32),
             vmem((n_acq // 2 * WIDE, COLS), F32),
@@ -502,12 +501,19 @@
         ),
     )(pltpu.with_memory_space_constraint(samples, pltpu.HBM), pltpu.with_memory_space_constraint(pair_live.T, pltpu.HBM))
     return pl.pallas_call(
-        place_out,
-        out_shape=tuple(jax.ShapeDtypeStruct(r.shape, F32) for r in results),
-        in_specs=[pl.BlockSpec(memory_space=pl.ANY)] * 2,
+        finish,
+        out_shape=(
+            jax.ShapeDtypeStruct((LOCAL, 2, ROWS, COLS), F32),
+            jax.ShapeDtypeStruct((LOCAL, LAGS, 2, ROWS, COLS), F32),
+        ),
+        in_specs=[pl.BlockSpec(memory_space=pltpu.VMEM)] * 3,
         out_specs=(pl.BlockSpec(memory_space=pl.ANY),) * 2,
-        scratch_shapes=[pltpu.SemaphoreType.DMA((LOCAL + 1,))],
-        compiler_params=pltpu.CompilerParams(vmem_limit_bytes=4 * 1024 * 1024),
+        scratch_shapes=[
+            vmem((LOCAL, 2, ROWS, COLS), F32),
+            vmem((LOCAL, LAGS, 2, ROWS, COLS), F32),
+            pltpu.SemaphoreType.DMA((LOCAL + 1,)),
+        ],
+        compiler_params=pltpu.CompilerParams(vmem_limit_bytes=8 * 1024 * 1024),
     )(*results)
 
 

time: 42.6 us -> 42.4 us (level)
  no operation moved by 1% of the time
where the time goes in v7:
time: 42.4 us; the launch traced here: 42.2 us
  Pallas kernels  41.6 us (98%)
  between operations  0.64 us (2%)
    pallas_call x1, Pallas kernels, per_device(): pl.pallas_call(functools.partial(kernel, n_acq, n_col), out_shape=(jax.Sh...  40.5 us
    pallas_call x1, Pallas kernels, per_device(): pl.pallas_call(finish, out_shape=(jax.ShapeDtypeStruct((LOCAL, 2, ROWS, C...  1.09 us

profile of v7, /device:TPU:1, one launch (start us, length us, event | category | flops | bytes accessed | tf_op | source)
XLA Modules:
  0.0 42.2 jit_solution(2265125925827948857)
XLA Ops:
  0.6 40.5 %shard_map.41 = (f32[2,16,24,128]{3,2,1,0:T(8,128)S(1)}, f32[4,12,2,24,128]{4,3,2,1,0:T(8,128)S(1)}, f32[48,8,128]{2,1,0:T(8,128)S(1)}) custom-call(f32[4,2,24,128]{3,2,1,0:T(8,128)} %x_hbm.1, s32[12,128]{1,0:T(8,128)} %bitcast.1), custom_call_target="tpu_custom_call" | custom-call | tf_op jit(solution)/shard_map/pallas_call | solution.py:460
  41.1 1.1 %shard_map.42 = (f32[4,2,24,128]{3,2,1,0:T(8,128)}, f32[4,12,2,24,128]{4,3,2,1,0:T(8,128)}) custom-call(f32[2,16,24,128]{3,2,1,0:T(8,128)S(1)} %get-tuple-element.5.disp, f32[4,12,2,24,128]{4,3,2,1,0:T(8,128)S(1)} %get-tuple-element.6.seen, f32[48,8,128]{2,1,0:T(8,128)S(1)} %get-tuple-element.7.flags), custom_call_target="tpu_custom_call" | custom-call | tf_op jit(solution)/shard_map/pallas_call | solution.py:503
